TPU v7x, 32 devices: a whole 2x2x4 slice. The times are simulated.
32 devices in a mesh: dp: 16 (over z, y, core), seq: 2 (over x).
Axes of the slice: x: 2, y: 2, z: 4, core: 2. Of those that a mesh axis runs over, the one named last changes fastest.
Arguments:
- tile_feats: bfloat16 [8192, 2048], P('dp'), may hold values from -6 to 6
- tile_pos: int32 [16, 512], P('dp'), may hold values from -1 to 511, as said below
- slide_count: int32 [16], P('dp'), may hold values from 128 to 512, as said below
- w_proj: bfloat16 [2048, 768], P(None, 'seq'), may hold values from -0.125 to 0.125
- emb_grad: bfloat16 [16, 512, 768], P('dp', 'seq'), may hold values from -6 to 6
- ln_gain: float32 [768], replicated, may hold values from 0.25 to 1.75
- w_qkv: bfloat16 [768, 2304], P('dp'), may hold values from -1.5 to 1.5
- w_out: bfloat16 [768, 768], P('dp'), may hold values from -0.21875 to 0.21875
Outputs:
- slide_emb: bfloat16 [16, 512, 768], P('dp', 'seq')
- attn_branch: bfloat16 [16, 512, 768], P('dp', 'seq')
- proj_grad: float32 [2048, 768], P(None, 'seq')
Inputs may be any that keep to these rules, and one draw needn't show every extreme that they name: `tile_pos`: slot j of a row belongs to slide j // 32. Each position below a slide's slide_count is held by exactly one slot of that slide over all rows; all other slots hold -1. `slide_count`: some slide is full.
All inputs are finite; a program needn't handle non-finite values.
Results may differ from a plain program's by a relative error of at most 0.017.
The roundings to bfloat16 on the way count: a program that leaves them out, or rounds other values in their place, can miss the bound.
Values may be sent and summed in bfloat16 or wider, within the bound.
A program may use at most 128 MiB of HBM per device.

v0:
```python
import functools

import jax
import jax.numpy as jnp
from jax import lax
from jax.experimental import pallas as pl
from jax.experimental.pallas import tpu as pltpu
from jax.sharding import PartitionSpec as P

D = 768
HEAD_COUNT = 12
HEAD_WIDTH = 64
DILATION_STEP = 4
NEGATIVE = -1e30
EPSILON = 1e-05
STEP_HEADS = 4

F32 = jnp.float32
BF16 = jnp.bfloat16
MESH = pl.DeviceIdType.MESH


def greet(dp_peers, seq_peers):
    barrier = pltpu.get_barrier_semaphore()
    dp_count, seq_count = lax.axis_size("dp"), lax.axis_size("seq")
    dp, seq = lax.axis_index("dp"), lax.axis_index("seq")
    if dp_peers:

        @pl.loop(1, dp_count)
        def _(t):
            pl.semaphore_signal(
                barrier, device_id=(lax.rem(dp + t, dp_count), seq), device_id_type=MESH
            )

    if seq_peers:

        @pl.loop(1, seq_count)
        def _(t):
            pl.semaphore_signal(
                barrier, device_id=(dp, lax.rem(seq + t, seq_count)), device_id_type=MESH
            )

    pl.semaphore_wait(
        barrier, (dp_count - 1 if dp_peers else 0) + (seq_count - 1 if seq_peers else 0)
    )


def remote(src, dst, send, recv, device):
    return pltpu.make_async_remote_copy(
        src_ref=src,
        dst_ref=dst,
        send_sem=send,
        recv_sem=recv,
        device_id=device,
        device_id_type=MESH,
    )


def dispatch_kernel(
    n, seq_count, pos, grad, emb, pos_out, emb_out, grad_out, grad_rows, picked, *sems
):
    ps, pr, xs, xr, es, er, gs, gr, fs, fr = sems
    dp, seq = lax.axis_index("dp"), lax.axis_index("seq")
    most = pos.shape[2]
    nearby, width = grad.shape[1:]
    greet(True, True)

    def column_copy(t):
        peer = lax.rem(seq + t, seq_count)
        return remote(grad.at[peer], grad_rows.at[seq], xs.at[t], xr.at[t], (dp, peer))

    def pos_copy(t):
        peer = lax.rem(dp + t, n)
        return remote(pos.at[peer], pos_out.at[dp], ps.at[t], pr.at[t], (peer, seq))

    def emb_copy(t):
        peer = lax.rem(dp + t, n)
        return remote(emb.at[peer], emb_out.at[seq, dp], es.at[t], er.at[t], (peer, seq))

    def grad_copy(t):
        peer = lax.rem(dp + t, n)
        return remote(picked.at[peer], grad_out.at[dp], gs.at[t], gr.at[t], (peer, seq))

    def forward(k, t):
        source = lax.rem(dp - t + n, n)
        peer = lax.rem(seq + k, seq_count)
        block = emb_out.at[seq, source]
        return remote(block, block, fs.at[k, t], fr.at[k, t], (dp, peer))

    @pl.loop(1, seq_count)
    def _(t):
        column_copy(t).start()

    @pl.loop(1, n)
    def _(t):
        pos_copy(t).start()

    @pl.loop(1, n)
    def _(t):
        emb_copy(t).start()

    pos_out[dp] = pos[dp]
    grad_rows[seq] = grad[seq]
    emb_out[seq, dp] = emb[dp]

    @pl.loop(1, n)
    def _(t):
        pos_copy(t).wait()

    @pl.loop(1, seq_count)
    def _(t):
        column_copy(t).wait()

    rows = jnp.concatenate([grad_rows[i] for i in range(seq_count)], axis=0)
    spot = lax.broadcasted_iota(jnp.int32, (nearby * seq_count, 1), 0)
    batch = 4
    for first in range(0, n, batch):
        at = jnp.concatenate([pos_out[first + i] for i in range(batch)], axis=1)
        hot = jnp.where(spot == at, 1.0, 0.0).astype(BF16)
        block = lax.dot_general(
            hot, rows, (((0,), (0,)), ((), ())), preferred_element_type=F32
        ).astype(BF16)
        for i in range(batch):
            picked[first + i] = block[i * most : (i + 1) * most]

    @pl.loop(1, n)
    def _(t):
        grad_copy(t).start()

    grad_out[dp] = picked[dp]
    for k in range(1, seq_count):
        forward(k, 0).start()

    @pl.loop(1, n)
    def _(t):
        emb_copy(t).wait_recv()
        for k in range(1, seq_count):
            forward(k, t).start()

    @pl.loop(1, n)
    def _(t):
        emb_copy(t).wait_send()
        grad_copy(t).wait()

    @pl.loop(0, n)
    def _(t):
        for k in range(1, seq_count):
            forward(k, t).wait()


def reduce_kernel(n, feats, slots, out, src, pair, cross, stage_b, stage_c, arrive, *sems):
    s1, r1, s2, r2, s3, r3, s4, r4, s5, r5, s6, r6 = sems
    dp, seq = lax.axis_index("dp"), lax.axis_index("seq")
    q = n // 4
    a, b, c = lax.rem(dp, 2), lax.rem(dp // 2, 2), dp // 4
    sibling = (dp + 1 - 2 * a, seq)
    across = (dp + 2 - 4 * b, seq)
    barrier = pltpu.get_barrier_semaphore()
    pl.semaphore_signal(barrier, device_id=sibling, device_id_type=MESH)
    pl.semaphore_signal(barrier, device_id=across, device_id_type=MESH)

    def ahead(t):
        return lax.rem(c + t, q)

    def behind(t):
        return lax.rem(c - t + q, q)

    def along(t):
        return (ahead(t) * 4 + b * 2 + a, seq)

    @pl.loop(1, q)
    def _(t):
        pl.semaphore_signal(barrier, device_id=along(t), device_id_type=MESH)

    rows = src.shape[3]
    tile = 512
    for first in range(0, n * rows, tile):
        product = lax.dot_general(
            feats[:, first : first + tile],
            slots[...],
            (((0,), (0,)), ((), ())),
            preferred_element_type=F32,
        ).astype(BF16)
        for i in range(tile // rows):
            k = first // rows + i
            src[k // (2 * q), k // q % 2, k % q] = product[i * rows : (i + 1) * rows]

    pl.semaphore_wait(barrier, q + 1)

    def side(i):
        return 1 - b if i == 0 else b

    def to_sibling(i, t):
        return remote(
            src.at[1 - a, side(i), ahead(t)], pair.at[i, t], s1.at[i, t], r1.at[i, t], sibling
        )

    def to_across(t):
        return remote(stage_b.at[t], cross.at[t], s2.at[t], r2.at[t], across)

    def to_owner(t):
        return remote(stage_c.at[t], arrive.at[t], s3.at[t], r3.at[t], along(t))

    def result_along(t):
        block = out.at[a, b, c]
        return remote(block, block, s4.at[t], r4.at[t], along(t))

    def result_across(t):
        block = out.at[a, b, behind(t)]
        return remote(block, block, s5.at[t], r5.at[t], across)

    def result_sibling(i, t):
        block = out.at[a, side(i), behind(t)]
        return remote(block, block, s6.at[i, t], r6.at[i, t], sibling)

    for i in (0, 1):

        @pl.loop(1, q + 1)
        def _(t):
            to_sibling(i, lax.rem(t, q)).start()

    @pl.loop(1, q + 1)
    def _(step):
        t = lax.rem(step, q)
        to_sibling(0, t).wait_recv()
        stage_b[t] = (src[a, 1 - b, ahead(t)].astype(F32) + pair[0, t].astype(F32)).astype(BF16)
        to_across(t).start()

    @pl.loop(1, q + 1)
    def _(step):
        t = lax.rem(step, q)
        to_sibling(1, t).wait_recv()
        to_across(t).wait_recv()
        stage_c[t] = (
            src[a, b, ahead(t)].astype(F32) + pair[1, t].astype(F32) + cross[t].astype(F32)
        ).astype(BF16)

        @pl.when(step < q)
        def _():
            to_owner(t).start()

    total = stage_c[0].astype(F32)
    for t in range(1, q):
        to_owner(t).wait_recv()
        total = total + arrive[t].astype(F32)
    out[a, b, c] = total.astype(BF16)

    @pl.loop(1, q)
    def _(t):
        result_along(t).start()

    result_across(0).start()
    result_sibling(1, 0).start()

    @pl.loop(1, q)
    def _(t):
        result_along(t).wait_recv()
        result_across(t).start()
        result_sibling(1, t).start()

    @pl.loop(0, q)
    def _(t):
        result_across(t).wait_recv()
        result_sibling(0, t).start()

    @pl.loop(1, q)
    def _(t):
        to_owner(t).wait_send()
        result_along(t).wait_send()

    for i in (0, 1):

        @pl.loop(0, q)
        def _(t):
            to_sibling(i, t).wait_send()
            result_sibling(i, t).wait()

    @pl.loop(0, q)
    def _(t):
        to_across(t).wait_send()
        result_across(t).wait_send()


VM = pl.BlockSpec(memory_space=pltpu.VMEM)
DMA = pltpu.SemaphoreType.DMA


def exchange(kernel, ident, outs, scratch, *operands):
    return pl.pallas_call(
        kernel,
        out_shape=tuple(jax.ShapeDtypeStruct(shape, kind) for shape, kind in outs),
        in_specs=[VM] * len(operands),
        out_specs=tuple([VM] * len(outs)),
        scratch_shapes=scratch,
        compiler_params=pltpu.CompilerParams(
            collective_id=ident, has_side_effects=True, vmem_limit_bytes=32 * 1024 * 1024
        ),
        cost_estimate=pl.CostEstimate(
            flops=10_000_000_000, bytes_accessed=10_000_000, transcendentals=0
        ),
    )(*operands)


def put_rows(whole, rows, low, high):
    pieces = [whole[:low]] if low else []
    pieces.append(rows)
    if high < whole.shape[0]:
        pieces.append(whole[high:])
    return jnp.concatenate(pieces, axis=0)


def attention_kernel(
    seq_count,
    nearby,
    meta_ref,
    rows_ref,
    gain_ref,
    wq_ref,
    wk_ref,
    wv_ref,
    wo_ref,
    emb_ref,
    branch_ref,
    normed,
    context,
):
    step = pl.program_id(0)
    me = meta_ref[0]
    count = meta_ref[1]
    part = nearby // DILATION_STEP
    own = pl.multiple_of(me * nearby, nearby)

    @pl.when(step == 0)
    def _():
        for block in range(seq_count):
            at = slice(block * nearby, (block + 1) * nearby)
            wide = jnp.concatenate(
                [rows_ref[c, at, :] for c in range(seq_count)], axis=-1
            ).astype(F32)
            center = jnp.mean(wide, axis=-1, keepdims=True)
            spread = jnp.mean(jnp.square(wide - center), axis=-1, keepdims=True)
            normed[at, :] = (
                (wide - center) * lax.rsqrt(spread + EPSILON) * gain_ref[...]
            ).astype(BF16)

    mine = normed[pl.ds(own, nearby), :]
    query = jnp.dot(mine, wq_ref[...], preferred_element_type=F32).astype(BF16)
    query = query * BF16(HEAD_WIDTH**-0.5)
    key = jnp.dot(mine, wk_ref[...], preferred_element_type=F32).astype(BF16)
    value = jnp.dot(mine, wv_ref[...], preferred_element_type=F32).astype(BF16)
    far_keys, far_values = [], []
    for other in range(1, seq_count):
        block = lax.rem(me + other, seq_count)
        start = pl.multiple_of(block * nearby, nearby)
        theirs = normed[pl.ds(start, nearby), :]
        far_keys.append(jnp.dot(theirs, wk_ref[...], preferred_element_type=F32).astype(BF16))
        far_values.append(jnp.dot(theirs, wv_ref[...], preferred_element_type=F32).astype(BF16))

    lane = lax.broadcasted_iota(jnp.int32, (1, nearby), 1)
    key_ok = own + (lane % part) * DILATION_STEP + lane // part < count
    row = lax.broadcasted_iota(jnp.int32, (nearby, 1), 0)
    query_ok = own + (row % part) * DILATION_STEP + row // part < count
    far_lane = lax.broadcasted_iota(jnp.int32, (1, part * (seq_count - 1)), 1)
    far_block = lax.rem(me + 1 + far_lane // part, seq_count)
    far_spot = far_block * nearby + far_lane % part * DILATION_STEP
    dims = (((1,), (1,)), ((), ()))
    outs = []
    for head in range(STEP_HEADS):
        shift = head % DILATION_STEP
        cols = slice(head * HEAD_WIDTH, (head + 1) * HEAD_WIDTH)
        low, high = shift * part, (shift + 1) * part
        q, k, v = query[:, cols], key[:, cols], value[:, cols]
        scores = lax.dot_general(q, k, dims, preferred_element_type=F32)
        scores = jnp.where(key_ok, scores, NEGATIVE)
        maximum = jnp.max(scores, axis=-1, keepdims=True)
        far_k = jnp.concatenate([x[low:high, cols] for x in far_keys], axis=0)
        far_v = jnp.concatenate([x[low:high, cols] for x in far_values], axis=0)
        far_ok = far_spot + shift < count
        far = lax.dot_general(q[low:high], far_k, dims, preferred_element_type=F32)
        far = jnp.where(far_ok, far, NEGATIVE)
        far_max = jnp.maximum(maximum[low:high], jnp.max(far, axis=-1, keepdims=True))
        maximum = put_rows(maximum, far_max, low, high)
        weight = jnp.exp(scores - maximum)
        in_lane = (lane >= low) & (lane < high)
        twice = jnp.where(in_lane, weight[low:high] * 2.0, weight[low:high])
        weight = put_rows(weight, twice, low, high)
        far_weight = jnp.exp(far - far_max)
        total = jnp.sum(weight, axis=-1, keepdims=True)
        far_total = jnp.sum(far_weight, axis=-1, keepdims=True)
        total = put_rows(total, total[low:high] + far_total, low, high)
        gathered = jnp.dot(weight.astype(BF16), v, preferred_element_type=F32)
        far_gathered = jnp.dot(far_weight.astype(BF16), far_v, preferred_element_type=F32)
        gathered = put_rows(gathered, gathered[low:high] + far_gathered, low, high)
        outs.append(jnp.where(query_ok, gathered / total, 0.0).astype(BF16))
    context[step] = jnp.concatenate(outs, axis=-1)

    @pl.when(step == pl.num_programs(0) - 1)
    def _():
        at_row = lax.broadcasted_iota(jnp.int32, (nearby, nearby), 0)
        at_lane = lax.broadcasted_iota(jnp.int32, (nearby, nearby), 1)
        natural = (at_lane % part) * DILATION_STEP + at_lane // part
        back = jnp.where(at_row == natural, 1.0, 0.0).astype(BF16)
        ordered = jnp.concatenate(
            [rows_ref[c, pl.ds(own, nearby), :] for c in range(seq_count)], axis=-1
        )
        emb_ref[...] = jnp.dot(back, ordered, preferred_element_type=F32).astype(BF16)
        whole = jnp.concatenate(
            [context[i] for i in range(HEAD_COUNT // STEP_HEADS)], axis=-1
        )
        whole = jnp.dot(back, whole, preferred_element_type=F32).astype(BF16)
        branch_ref[...] = jnp.dot(whole, wo_ref[...], preferred_element_type=F32).astype(BF16)


def attend(meta, rows, gain, weights, seq_count, nearby):
    width = STEP_HEADS * HEAD_WIDTH
    steps = HEAD_COUNT // STEP_HEADS
    slide_len = rows.shape[1]
    full = lambda *shape: pl.BlockSpec(shape, lambda i: (0,) * len(shape))
    out = jax.ShapeDtypeStruct((nearby, D), BF16)
    return pl.pallas_call(
        functools.partial(attention_kernel, seq_count, nearby),
        out_shape=(out, out),
        grid=(steps,),
        in_specs=[
            pl.BlockSpec(memory_space=pltpu.SMEM),
            full(*rows.shape),
            full(1, D),
            pl.BlockSpec((D, width), lambda i: (0, i)),
            pl.BlockSpec((D, width), lambda i: (0, steps + i)),
            pl.BlockSpec((D, width), lambda i: (0, 2 * steps + i)),
            pl.BlockSpec((D, D), lambda i: (0, 3)),
        ],
        out_specs=(full(nearby, D), full(nearby, D)),
        scratch_shapes=[
            pltpu.VMEM((slide_len, D), BF16),
            pltpu.VMEM((steps, nearby, width), BF16),
        ],
        compiler_params=pltpu.CompilerParams(vmem_limit_bytes=60 * 1024 * 1024),
        cost_estimate=pl.CostEstimate(
            flops=20_000_000_000, bytes_accessed=20_000_000, transcendentals=1_000_000
        ),
    )(meta, rows, gain, weights, weights, weights, weights)


def local(tile_feats, tile_pos, slide_count, w_proj, emb_grad, ln_gain, w_qkv, w_out):
    seq_count = lax.axis_size("seq")
    n = lax.axis_size("dp")
    seq_index = lax.axis_index("seq")
    slot_rows = tile_feats.shape[0]
    nearby = emb_grad.shape[1]
    slide_len = nearby * seq_count
    part = nearby // DILATION_STEP
    most = slot_rows // n
    width = w_proj.shape[1]
    weights = lax.all_gather(
        jnp.concatenate([w_qkv, w_out], axis=1), "dp", axis=0, tiled=True
    )
    emb_part = jnp.dot(tile_feats, w_proj, preferred_element_type=F32).astype(BF16)
    positions, arrived, slot_grad = exchange(
        functools.partial(dispatch_kernel, n, seq_count),
        1,
        [
            ((n, 1, most), jnp.int32),
            ((seq_count, n, most, width), BF16),
            ((n, most, width), BF16),
        ],
        [pltpu.VMEM((seq_count, nearby, width), BF16), pltpu.VMEM((n, most, width), BF16)]
        + [DMA((n,))] * 2
        + [DMA((seq_count,))] * 2
        + [DMA((n,))] * 4
        + [DMA((seq_count, n))] * 2,
        tile_pos.reshape(n, 1, most),
        emb_grad.reshape(nearby, seq_count, width).transpose(1, 0, 2),
        emb_part.reshape(n, most, width),
    )
    positions = positions.reshape(slot_rows)
    spot = jnp.arange(slide_len, dtype=jnp.int32)
    features = tile_feats.shape[1]
    quarter = n // 4
    shape = (2, 2, quarter, features // n, width)
    (summed,) = exchange(
        functools.partial(reduce_kernel, n),
        3,
        [(shape, BF16)],
        [pltpu.VMEM(shape, BF16), pltpu.VMEM(shape[1:], BF16)]
        + [pltpu.VMEM(shape[2:], BF16)] * 4
        + [DMA((2, quarter))] * 2
        + [DMA((quarter,))] * 8
        + [DMA((2, quarter))] * 2,
        tile_feats,
        slot_grad.reshape(slot_rows, width),
    )
    proj_grad = summed.reshape(features, width).astype(F32)

    inside = spot % nearby
    at_spot = spot - inside + (inside % part) * DILATION_STEP + inside // part
    hot_perm = (at_spot[:, None] == positions[None, :]).astype(BF16)
    rows = jnp.einsum(
        "ps,csw->cpw",
        hot_perm,
        arrived.reshape(seq_count, slot_rows, width),
        preferred_element_type=F32,
    ).astype(BF16)
    meta = jnp.stack([seq_index.astype(jnp.int32), slide_count[0]])
    local_emb, attn_branch = attend(
        meta, rows, ln_gain.reshape(1, D), weights, seq_count, nearby
    )
    return (local_emb[None], attn_branch[None], proj_grad)


def solution(mesh):
    in_specs = (
        P("dp", None),
        P("dp", None),
        P("dp"),
        P(None, "seq"),
        P("dp", "seq", None),
        P(),
        P("dp", None),
        P("dp", None),
    )
    out_specs = (P("dp", "seq", None), P("dp", "seq", None), P(None, "seq"))
    return jax.shard_map(local, mesh=mesh, in_specs=in_specs, out_specs=out_specs, check_vma=False)
```

profile of v0, /device:TPU:0, one launch (start us, length us, event | category | flops | bytes accessed | tf_op | source)
XLA Modules:
  0.0 118.5 jit_solution(18147766462240013665)
XLA Ops:
  7.2 0.0 copy-start
  7.2 0.0 all-gather.2.cloned.1.call-start
  7.2 1.8 %pad_maximum_fusion = bf16[48,3072]{1,0:T(8,128)(2,1)} fusion(bf16[48,768]{1,0:T(8,128)(2,1)} %param.15, bf16[48,2304]{1,0:T(8,128)(2,1)} %param.14), kind=kLoop, calls=%fused_computation.8 | loop fusion | flops 589824 | bytes 589824 | tf_op jit(solution)/shard_map/concatenate | solution.py:456
  9.0 0.0 all-gather.2.cloned.1.call-update
  9.1 0.5 broadcast.83
  9.6 1.3 %reduce.6 = s32[512]{0:T(512)S(1)} reduce(s32[1,512]{1,0:T(1,128)} %param.9, s32[]{:T(128)} %broadcast.83), dimensions={0}, to_apply=%param.9.reduce_sub_computation.3 | reduce | bytes 4100 | tf_op args[1]
  10.9 0.1 reshape.68.pos
  11.0 1.2 copy.13
  12.2 0.2 copy.14
  12.4 0.0 copy-done
  12.4 2.8 %convolution_convert_fusion.1 = bf16[512,384]{1,0:T(8,128)(2,1)S(1)} fusion(bf16[512,2048]{1,0:T(8,128)(2,1)} %feats.1, bf16[2048,384]{1,0:T(8,128)(2,1)S(1)} %copy-done), kind=kOutput, calls=%fused_computation.3 | convolution fusion | flops 805502976 | bytes 4063232 | tf_op jit(solution)/shard_map/dot_general | solution.py:458
  15.3 0.0 copy-start.2
  15.3 32.7 %shard_map.103 = (s32[16,1,32]{2,1,0:T(1,128)S(1)}, bf16[2,16,32,384]{3,2,1,0:T(8,128)(2,1)S(1)}, bf16[16,32,384]{2,1,0:T(8,128)(2,1)S(1)}) custom-call(s32[16,1,32]{2,1,0:T(1,128)S(1)} %reshape.68.pos, bf16[2,256,384]{2,1,0:T(8,128)(2,1)S(1)} %bitcast.19, bf16[16,32,384]{2,1,0:T(8,128)(2,1)S(1)} %bitcast.22), custom_call_target="tpu_custom_call" | custom-call | flops 10000000000 | bytes 10000000 | tf_op jit(solution)/shard_map/pallas_call | solution.py:289
  48.0 0.7 reduce.7
  48.7 0.1 eq.19
  48.8 0.0 copy-done.2
  48.8 0.6 reshape.72.gain_ref
  49.4 0.0 copy-start.1
  50.2 0.7 pad_add_fusion.meta_ref
  50.8 1.5 %fusion.rows_ref = bf16[2,512,384]{2,1,0:T(8,128)(2,1)} fusion(bf16[2,512,384]{2,1,0:T(8,128)(2,1)S(1)} %bitcast.20, s32[512]{0:T(512)S(1)} %eq.19, s32[512]{0:T(512)S(1)} %fusion.11), kind=kOutput, calls=%fused_computation.2 | convolution fusion | flops 403308544 | bytes 1576960 | tf_op jit(solution)/shard_map/ps,csw->cpw/dot_general | solution.py:498
  52.3 0.0 copy-done.1
  52.4 45.6 %shard_map.105 = bf16[2,2,4,128,384]{4,3,2,1,0:T(8,128)(2,1)S(1)} custom-call(bf16[512,2048]{1,0:T(8,128)(2,1)S(1)} %copy-done.1, bf16[512,384]{1,0:T(8,128)(2,1)S(1)} %bitcast.21), custom_call_target="tpu_custom_call" | custom-call | flops 10000000000 | bytes 10000000 | tf_op jit(solution)/shard_map/pallas_call | solution.py:289
  98.0 2.0 %bitcast_convert_fusion = f32[2048,384]{1,0:T(8,128)} fusion(bf16[2,2,4,128,384]{4,3,2,1,0:T(8,128)(2,1)S(1)} %shard_map.105), kind=kLoop, calls=%fused_computation | loop fusion | flops 786432 | bytes 4718592 | tf_op jit(solution)/shard_map/convert_element_type | solution.py:493
  100.0 0.0 all-gather.2.cloned.1.call-done.wq_ref.wk_ref.wv_ref.wo_ref
  100.0 11.6 %shard_map.104 = (bf16[256,768]{1,0:T(8,128)(2,1)}, bf16[256,768]{1,0:T(8,128)(2,1)}) custom-call(s32[2]{0:T(128)} %pad_add_fusion.meta_ref, bf16[2,512,384]{2,1,0:T(8,128)(2,1)} %fusion.rows_ref, f32[1,768]{1,0:T(1,128)} %reshape.72.gain_ref, bf16[768,3072]{1,0:T(8,128)(2,1)} %all-gather.2.cloned.1.call-done.wq_ref.wk_ref.wv_ref.wo_ref, ...), custom_call_target="tpu_custom_call" | custom-call | flops 20000000000 | bytes 20000000 | tf_op jit(solution)/shard_map/pallas_call | solution.py:420
  (1 shorter events, 0.0 us)
Async XLA Ops:
  7.2 5.2 %copy-start = (bf16[2048,384]{1,0:T(8,128)(2,1)S(1)}, bf16[2048,384]{1,0:T(8,128)(2,1)}, u32[]{:S(2)}) copy-start(bf16[2048,384]{1,0:T(8,128)(2,1)} %param.11) | copy-start | bytes 4718596
  7.2 92.8 %all-gather.2.cloned.1.call-start = ((), (), s32[]{:S(2)}) async-start(), calls=%async_computation | async-start | bytes 5013504 | tf_op jit(solution)/shard_map/all_gather | solution.py:455
  15.3 33.5 %copy-start.2 = (f32[768]{0:T(1024)S(1)}, f32[768]{0:T(1024)}, u32[]{:S(2)}) copy-start(f32[768]{0:T(1024)} %param.13) | copy-start | bytes 9220
  49.4 3.0 %copy-start.1 = (bf16[512,2048]{1,0:T(8,128)(2,1)S(1)}, bf16[512,2048]{1,0:T(8,128)(2,1)}, u32[]{:S(2)}) copy-start(bf16[512,2048]{1,0:T(8,128)(2,1)} %feats.1) | copy-start | bytes 6291460
Sparse Core Ops, SparseCore 0:
  10.9 84.4 all-gather.1
where the time goes:
time: 119 us; the launch traced here: 118 us
  Pallas kernels  90 us (76%)
  between operations  14.9 us (13%)
  other arithmetic  6.53 us (5%)
  matrix products  4.35 us (4%)
  local copies, waits for them, and re-layouts  2.67 us (2%)
    pallas_call x2, Pallas kernels, exchange(): pl.pallas_call(kernel, out_shape=tuple((jax.ShapeDtypeStruct(shape, kind)...  78.4 us
    pallas_call x1, Pallas kernels, attend(): pl.pallas_call(functools.partial(attention_kernel, seq_count, nearby), ou...  11.6 us
    dot_general x1, matrix products, local(): jnp.dot(tile_feats, w_proj, preferred_element_type=F32).astype(BF16)  2.84 us
  transfers between devices with their start and end apart: 1, of which 0 were waited for; matrix products, arithmetic and copies ran while one was open for 10% of the time, Pallas kernels for 66%

commit v1 on v0

--- a/solution.py
+++ b/solution.py
@@ -508,6 +508,678 @@
     return (local_emb[None], attn_branch[None], proj_grad)
 
 
+ROUNDS = 2
+ANY = pl.BlockSpec(memory_space=pl.ANY)
+NT = (((1,), (1,)), ((), ()))
+TN = (((0,), (0,)), ((), ()))
+
+
+def split_first(count):
+    size = count // ROUNDS
+    return [pl.ds(r * size, size) for r in range(ROUNDS)]
+
+
+def fused_kernel(
+    n,
+    feats_hbm,
+    pos,
+    slide_count,
+    wproj_hbm,
+    grad,
+    gain,
+    wqkv,
+    wout,
+    emb_ref,
+    branch_ref,
+    out,
+    feats,
+    wproj,
+    emb,
+    pos_in,
+    pos_all,
+    emb_all,
+    grad_rows,
+    picked,
+    slots,
+    wts,
+    wts_x,
+    normed,
+    qkv,
+    ctx_send,
+    ctx_own,
+    ctx_peer,
+    src,
+    pair,
+    cross,
+    stage_b,
+    stage_c,
+    arrive,
+    local_sems,
+    xs,
+    xr,
+    ps,
+    pr,
+    es,
+    er,
+    fs,
+    fr,
+    gs,
+    gr,
+    us,
+    ur,
+    ds_,
+    dr,
+    ys,
+    yr,
+    cs,
+    cr,
+    wxs,
+    wxr,
+    ks,
+    kr,
+    s1,
+    r1,
+    s2,
+    r2,
+    s3,
+    r3,
+    s4,
+    r4,
+    s5,
+    r5,
+    s6,
+    r6,
+):
+    dp, seq = lax.axis_index("dp"), lax.axis_index("seq")
+    q = n // 4
+    a, b, c = lax.rem(dp, 2), lax.rem(dp // 2, 2), dp // 4
+    x_peer = (dp, 1 - seq)
+    sib_dp = dp + 1 - 2 * a
+    y_dp = dp + 2 - 4 * b
+    sibling, across = (sib_dp, seq), (y_dp, seq)
+    most = pos_in.shape[2]
+    slot_rows = feats.shape[0]
+    nearby = grad.shape[1]
+    width = wproj.shape[1]
+    depth = wqkv.shape[0]
+    part = nearby // DILATION_STEP
+    inner = HEAD_COUNT * HEAD_WIDTH
+    wide = 3 * width
+
+    feats_copy = pltpu.make_async_copy(feats_hbm, feats, local_sems.at[0])
+    wproj_copy = pltpu.make_async_copy(wproj_hbm, wproj, local_sems.at[1])
+    wproj_copy.start()
+    feats_copy.start()
+    barrier = pltpu.get_barrier_semaphore()
+
+    @pl.loop(1, n)
+    def _(t):
+        pl.semaphore_signal(barrier, device_id=(lax.rem(dp + t, n), seq), device_id_type=MESH)
+
+    pl.semaphore_signal(barrier, device_id=x_peer, device_id_type=MESH)
+
+    for i in range(n):
+        pos_in[i] = pos[:, i * most : (i + 1) * most]
+    mine_w = pl.ds(pl.multiple_of(dp * depth, 16), depth)
+    half = pl.multiple_of(seq * width, width)
+    for i in range(3):
+        wts[mine_w, i * width : (i + 1) * width] = wqkv[
+            :, pl.ds(pl.multiple_of(i * inner + half, 128), width)
+        ]
+    wts[mine_w, wide:] = wout[:, pl.ds(half, width)]
+    pos_all[dp] = pos_in[dp]
+
+    def column_copy():
+        block = grad.at[0, :, pl.ds(pl.multiple_of((1 - seq) * width, 128), width)]
+        return remote(block, grad_rows.at[seq], xs.at[0], xr.at[0], x_peer)
+
+    own_columns = pltpu.make_async_copy(
+        grad.at[0, :, pl.ds(half, width)], grad_rows.at[seq], local_sems.at[2]
+    )
+    own_columns.start()
+
+    def pos_copy(t):
+        peer = lax.rem(dp + t, n)
+        return remote(pos_in.at[peer], pos_all.at[dp], ps.at[t], pr.at[t], (peer, seq))
+
+    def emb_copy(t):
+        peer = lax.rem(dp + t, n)
+        return remote(
+            emb.at[pl.ds(pl.multiple_of(peer * most, most), most)],
+            emb_all.at[seq, dp],
+            es.at[t],
+            er.at[t],
+            (peer, seq),
+        )
+
+    def forward(t):
+        block = emb_all.at[seq, lax.rem(dp - t + n, n)]
+        return remote(block, block, fs.at[t], fr.at[t], x_peer)
+
+    def grad_send(peer):
+        return remote(picked.at[peer], slots.at[dp], gs.at[peer], gr.at[dp], (peer, seq))
+
+    def grad_recv(source):
+        return remote(picked.at[source], slots.at[source], gs.at[source], gr.at[source], sibling)
+
+    pl.semaphore_wait(barrier, n)
+    column_copy().start()
+
+    @pl.loop(1, n)
+    def _(t):
+        pos_copy(t).start()
+
+    wproj_copy.wait()
+    feats_copy.wait()
+    emb[...] = jnp.dot(feats[...], wproj[...], preferred_element_type=F32).astype(BF16)
+
+    @pl.loop(1, n)
+    def _(t):
+        emb_copy(t).start()
+
+    emb_all[seq, dp] = emb[pl.ds(pl.multiple_of(dp * most, most), most), :]
+    forward(0).start()
+
+    @pl.loop(1, n)
+    def _(t):
+        pos_copy(t).wait()
+
+    own_columns.wait()
+    column_copy().wait()
+    rows = jnp.concatenate([grad_rows[0], grad_rows[1]], axis=0)
+    spot = lax.broadcasted_iota(jnp.int32, (2 * nearby, 1), 0)
+    batch = 4
+
+    @pl.loop(1, q + 1)
+    def _(step):
+        first = lax.rem(c + step, q) * batch
+        at = jnp.concatenate([pos_all[first + i] for i in range(batch)], axis=1)
+        hot = jnp.where(spot == at, 1.0, 0.0).astype(BF16)
+        block = lax.dot_general(hot, rows, TN, preferred_element_type=F32).astype(BF16)
+        for i in range(batch):
+            picked[first + i] = block[i * most : (i + 1) * most]
+
+            @pl.when(first + i != dp)
+            def _():
+                grad_send(first + i).start()
+
+            @pl.when(first + i == dp)
+            def _():
+                slots[first + i] = block[i * most : (i + 1) * most]
+
+    def rows_of(who):
+        return pl.ds(pl.multiple_of(who * depth, 16), depth)
+
+    def z_block(z):
+        return wts.at[rows_of(z * 4 + b * 2 + a)]
+
+    def up(hop, z):
+        return remote(z_block(z), z_block(z), us.at[hop], ur.at[hop], (lax.rem(dp + 4, n), seq))
+
+    def down(hop, z):
+        return remote(z_block(z), z_block(z), ds_.at[hop], dr.at[hop], (lax.rem(dp + n - 4, n), seq))
+
+    def y_copy(z, back=False):
+        who = z * 4 + (1 - b if back else b) * 2 + a
+        block = wts.at[rows_of(who)]
+        return remote(block, block, ys.at[z], yr.at[z], across)
+
+    def c_copy(side, z, back=False):
+        y = b if side == 0 else 1 - b
+        who = z * 4 + y * 2 + (1 - a if back else a)
+        block = wts.at[rows_of(who)]
+        return remote(block, block, cs.at[side, z], cr.at[side, z], sibling)
+
+    def w_start():
+        @pl.when(c < q - 1)
+        def _():
+            up(1, c).start()
+
+        @pl.when(c > 0)
+        def _():
+            down(1, c).start()
+
+        y_copy(c).start()
+        c_copy(0, c).start()
+
+    def w_hop(hop):
+        below, above = c - hop, c + hop
+
+        @pl.when(below >= 0)
+        def _():
+            up(hop, below).wait_recv()
+
+            @pl.when(c < q - 1)
+            def _():
+                up(hop + 1, below).start()
+
+            y_copy(below).start()
+            c_copy(0, below).start()
+
+        @pl.when(above < q)
+        def _():
+            down(hop, above).wait_recv()
+
+            @pl.when(c > 0)
+            def _():
+                down(hop + 1, above).start()
+
+            y_copy(above).start()
+            c_copy(0, above).start()
+
+    def w_side():
+        @pl.loop(0, q)
+        def _(t):
+            z = lax.rem(c + t, q)
+            y_copy(z, True).wait_recv()
+            c_copy(1, z).start()
+
+    def wx_copy():
+        return remote(wts.at[:, pl.ds(wide, width)], wts_x, wxs.at[0], wxr.at[0], x_peer)
+
+    def w_gathered():
+        @pl.loop(0, q)
+        def _(z):
+            c_copy(0, z, True).wait_recv()
+            c_copy(1, z, True).wait_recv()
+
+        wx_copy().start()
+
+    def w_done():
+        for hop in range(1, q):
+
+            @pl.when((c - hop + 1 >= 0) & (c < q - 1))
+            def _():
+                up(hop, c - hop + 1).wait_send()
+
+            @pl.when((c + hop - 1 < q) & (c > 0))
+            def _():
+                down(hop, c + hop - 1).wait_send()
+
+        @pl.loop(0, q)
+        def _(z):
+            y_copy(z).wait_send()
+            c_copy(0, z).wait_send()
+            c_copy(1, z).wait_send()
+
+        wx_copy().wait_send()
+
+    w_start()
+
+    @pl.loop(1, n)
+    def _(t):
+        emb_copy(t).wait_recv()
+        forward(t).start()
+
+    w_hop(1)
+    w_hop(2)
+
+    count = slide_count[0]
+    own = pl.multiple_of(seq * nearby, nearby)
+    far_own = pl.multiple_of((1 - seq) * nearby, nearby)
+    positions = jnp.concatenate([pos_all[i] for i in range(n)], axis=1)
+
+    def natural_of(index, shift):
+        return (index % part) * DILATION_STEP + lax.rem(index // part + 2 * shift, DILATION_STEP)
+
+    inside = spot % nearby
+    at_spot = spot - inside + natural_of(inside, seq)
+    hot_perm = jnp.where(at_spot == positions, 1.0, 0.0).astype(BF16)
+    own_spot = lax.broadcasted_iota(jnp.int32, (nearby, 1), 0) + seq * nearby
+    hot_own = jnp.where(own_spot == positions, 1.0, 0.0).astype(BF16)
+
+    @pl.loop(0, n)
+    def _(t):
+        forward(t).wait_recv()
+
+    def regroup():
+        blocks = [emb_all[i].reshape(slot_rows, width) for i in range(2)]
+        for i in range(2):
+            emb_ref[:, i * width : (i + 1) * width] = jnp.dot(
+                hot_own, blocks[i], preferred_element_type=F32
+            ).astype(BF16)
+        for block in range(2):
+            at = slice(block * nearby, (block + 1) * nearby)
+            row = jnp.concatenate(
+                [jnp.dot(hot_perm[at], blocks[i], preferred_element_type=F32) for i in range(2)],
+                axis=-1,
+            )
+            center = jnp.mean(row, axis=-1, keepdims=True)
+            spread = jnp.mean(jnp.square(row - center), axis=-1, keepdims=True)
+            normed[at, :] = (
+                (row - center) * lax.rsqrt(spread + EPSILON) * gain[...][None, :]
+            ).astype(BF16)
+
+    regroup()
+
+    ranges = split_first(src.shape[3])
+
+    def side(i):
+        return 1 - b if i == 0 else b
+
+    def ahead(t):
+        return lax.rem(c + t, q)
+
+    def behind(t):
+        return lax.rem(c - t + q, q)
+
+    def along(t):
+        return (ahead(t) * 4 + b * 2 + a, seq)
+
+    def to_sibling(r, i, t):
+        at = ranges[r]
+        return remote(
+            src.at[1 - a, side(i), ahead(t), at],
+            pair.at[i, t, at],
+            s1.at[r, i, t],
+            r1.at[r, i, t],
+            sibling,
+        )
+
+    def to_across(r, t):
+        at = ranges[r]
+        return remote(stage_b.at[t, at], cross.at[t, at], s2.at[r, t], r2.at[r, t], across)
+
+    def to_owner(r, t):
+        at = ranges[r]
+        return remote(stage_c.at[t, at], arrive.at[t, at], s3.at[r, t], r3.at[r, t], along(t))
+
+    def result_along(r, t):
+        block = out.at[a, b, c, ranges[r]]
+        return remote(block, block, s4.at[r, t], r4.at[r, t], along(t))
+
+    def result_across(r, t):
+        block = out.at[a, b, behind(t), ranges[r]]
+        return remote(block, block, s5.at[r, t], r5.at[r, t], across)
+
+    def result_sibling(r, i, t):
+        block = out.at[a, side(i), behind(t), ranges[r]]
+        return remote(block, block, s6.at[r, i, t], r6.at[r, i, t], sibling)
+
+    order = [t % q for t in range(1, q + 1)]
+
+    @pl.loop(0, n)
+    def _(source):
+        @pl.when(source != dp)
+        def _():
+            grad_recv(source).wait_recv()
+
+    rows_each = src.shape[3]
+    grads = slots[...].reshape(slot_rows, width)
+    tile = q * rows_each
+
+    @pl.loop(0, n // q)
+    def _(step):
+        core = lax.rem(1 - a + step // 2, 2)
+        y = lax.rem(1 - b + step, 2)
+        first = pl.multiple_of((core * 2 + y) * tile, tile)
+        product = lax.dot_general(
+            feats[:, pl.ds(first, tile)], grads, TN, preferred_element_type=F32
+        ).astype(BF16)
+        for i in range(q):
+            src[core, y, i] = product[i * rows_each : (i + 1) * rows_each]
+
+        for i in range(2):
+
+            @pl.when(step == i)
+            def _():
+                for r in range(ROUNDS):
+                    for t in order:
+                        to_sibling(r, i, t).start()
+
+    def sum_b(r, t):
+        to_sibling(r, 0, t).wait_recv()
+        at = ranges[r]
+        stage_b[t, at] = (
+            src[a, 1 - b, ahead(t), at].astype(F32) + pair[0, t, at].astype(F32)
+        ).astype(BF16)
+        to_across(r, t).start()
+
+    def sum_c(r, t):
+        to_sibling(r, 1, t).wait_recv()
+        to_across(r, t).wait_recv()
+        at = ranges[r]
+        stage_c[t, at] = (
+            src[a, b, ahead(t), at].astype(F32)
+            + pair[1, t, at].astype(F32)
+            + cross[t, at].astype(F32)
+        ).astype(BF16)
+        if t:
+            to_owner(r, t).start()
+
+    def own_sum(r):
+        at = ranges[r]
+        total = stage_c[0, at].astype(F32)
+        for t in range(1, q):
+            to_owner(r, t).wait_recv()
+            total = total + arrive[t, at].astype(F32)
+        out[a, b, c, at] = total.astype(BF16)
+        for t in range(1, q):
+            result_along(r, t).start()
+        result_across(r, 0).start()
+        result_sibling(r, 1, 0).start()
+
+    def result_on(r, t):
+        result_along(r, t).wait_recv()
+        result_across(r, t).start()
+        result_sibling(r, 1, t).start()
+
+    def result_over(r, t):
+        result_across(r, t).wait_recv()
+        result_sibling(r, 0, t).start()
+
+    def reduce_done():
+        for r in range(ROUNDS):
+
+            @pl.loop(0, q)
+            def _(t):
+                for i in range(2):
+                    to_sibling(r, i, t).wait_send()
+                    result_sibling(r, i, t).wait()
+                to_across(r, t).wait_send()
+                result_across(r, t).wait_send()
+
+            @pl.loop(1, q)
+            def _(t):
+                to_owner(r, t).wait_send()
+                result_along(r, t).wait_send()
+
+    lane = lax.broadcasted_iota(jnp.int32, (1, nearby), 1)
+    row_at = lax.broadcasted_iota(jnp.int32, (nearby, 1), 0)
+    far_lane = lax.broadcasted_iota(jnp.int32, (1, part), 1)
+
+    def project(which):
+        cols = slice(which * width, (which + 1) * width)
+        value = jnp.dot(normed[...], wts[:, cols], preferred_element_type=F32).astype(BF16)
+        if which == 0:
+            value = value * BF16(HEAD_WIDTH**-0.5)
+        qkv[which] = value
+
+    def attend_head(start, other, head):
+        group = head % DILATION_STEP
+        cols = slice(head * HEAD_WIDTH, (head + 1) * HEAD_WIDTH)
+        low, high = group * part, (group + 1) * part
+        key_ok = start + natural_of(lane, seq) < count
+        query_ok = start + natural_of(row_at, seq) < count
+        far_ok = (
+            other + far_lane * DILATION_STEP + lax.rem(group + 2 * seq, DILATION_STEP) < count
+        )
+        here = pl.ds(start, nearby)
+        there = pl.ds(pl.multiple_of(other + low, part), part)
+        qh, kh, vh = (qkv[i, here, :][:, cols] for i in range(3))
+        far_k, far_v = (qkv[i, there, :][:, cols] for i in (1, 2))
+        scores = lax.dot_general(qh, kh, NT, preferred_element_type=F32)
+        scores = jnp.where(key_ok, scores, NEGATIVE)
+        maximum = jnp.max(scores, axis=-1, keepdims=True)
+        far = lax.dot_general(qh[low:high], far_k, NT, preferred_element_type=F32)
+        far = jnp.where(far_ok, far, NEGATIVE)
+        far_max = jnp.maximum(maximum[low:high], jnp.max(far, axis=-1, keepdims=True))
+        maximum = put_rows(maximum, far_max, low, high)
+        weight = jnp.exp(scores - maximum)
+        in_lane = (lane >= low) & (lane < high)
+        twice = jnp.where(in_lane, weight[low:high] * 2.0, weight[low:high])
+        weight = put_rows(weight, twice, low, high)
+        far_weight = jnp.exp(far - far_max)
+        total = jnp.sum(weight, axis=-1, keepdims=True)
+        far_total = jnp.sum(far_weight, axis=-1, keepdims=True)
+        total = put_rows(total, total[low:high] + far_total, low, high)
+        gathered = jnp.dot(weight.astype(BF16), vh, preferred_element_type=F32)
+        far_gathered = jnp.dot(far_weight.astype(BF16), far_v, preferred_element_type=F32)
+        gathered = put_rows(gathered, gathered[low:high] + far_gathered, low, high)
+        return jnp.where(query_ok, gathered / total, 0.0).astype(BF16)
+
+    def ctx_copy(j):
+        at = pl.ds(j * 128, 128)
+        return remote(ctx_send.at[:, at], ctx_peer.at[:, at], ks.at[j], kr.at[j], x_peer)
+
+    pairs = width // 128
+
+    def heads(mine, j):
+        start, other = (own, far_own) if mine else (far_own, own)
+        block = jnp.concatenate(
+            [attend_head(start, other, 2 * j + i) for i in range(2)], axis=-1
+        )
+        at = pl.ds(j * 128, 128)
+        if mine:
+            ctx_own[:, at] = block
+        else:
+            ctx_send[:, at] = block
+            ctx_copy(j).start()
+
+    def finish_branch():
+        for j in range(pairs):
+            ctx_copy(j).wait()
+        wx_copy().wait_recv()
+        at_row = lax.broadcasted_iota(jnp.int32, (nearby, nearby), 0)
+        at_lane = lax.broadcasted_iota(jnp.int32, (nearby, nearby), 1)
+        ordered = []
+        for shift, ref in ((seq, ctx_own), (1 - seq, ctx_peer)):
+            back = jnp.where(at_row == natural_of(at_lane, shift), 1.0, 0.0).astype(BF16)
+            ordered.append(jnp.dot(back, ref[...], preferred_element_type=F32).astype(BF16))
+        for cols, weight in ((seq, wts.at[:, pl.ds(wide, width)]), (1 - seq, wts_x)):
+            total = None
+            for value, owner in zip(ordered, (seq, 1 - seq)):
+                at = pl.ds(pl.multiple_of(owner * width, width), width)
+                term = jnp.dot(value, weight[at, :], preferred_element_type=F32)
+                total = term if total is None else total + term
+            branch_ref[:, pl.ds(pl.multiple_of(cols * width, width), width)] = total.astype(BF16)
+
+    reduce_steps = []
+    for r in range(ROUNDS):
+        reduce_steps += [functools.partial(sum_b, r, t) for t in order]
+    for r in range(ROUNDS):
+        reduce_steps += [functools.partial(sum_c, r, t) for t in order]
+        reduce_steps += [functools.partial(own_sum, r)]
+        if r:
+            reduce_steps += [functools.partial(result_on, r - 1, t) for t in range(1, q)]
+            reduce_steps += [functools.partial(result_over, r - 1, t) for t in range(q)]
+    r = ROUNDS - 1
+    reduce_steps += [functools.partial(result_on, r, t) for t in range(1, q)]
+    reduce_steps += [functools.partial(result_over, r, t) for t in range(q)]
+
+    work = [functools.partial(project, i) for i in range(3)]
+    work += [functools.partial(heads, False, j) for j in range(pairs)]
+    work += [functools.partial(heads, True, j) for j in range(pairs)]
+
+    w_hop(3)
+    split = 2 * q
+    for step in reduce_steps[:q]:
+        step()
+    w_side()
+    for step in reduce_steps[q:split]:
+        step()
+    w_gathered()
+    rest = reduce_steps[split:]
+    slots_left = len(work)
+    taken = 0
+    for i, job in enumerate(work):
+        job()
+        until = (i + 1) * len(rest) // (slots_left + 2)
+        for step in rest[taken:until]:
+            step()
+        taken = until
+    finish_branch()
+    for step in rest[taken:]:
+        step()
+
+    @pl.loop(1, n)
+    def _(t):
+        emb_copy(t).wait_send()
+
+    @pl.loop(0, n)
+    def _(t):
+        forward(t).wait_send()
+
+        @pl.when(t != dp)
+        def _():
+            grad_send(t).wait_send()
+
+    w_done()
+    reduce_done()
+
+
+def fused(tile_feats, tile_pos, slide_count, w_proj, emb_grad, ln_gain, w_qkv, w_out):
+    n = lax.axis_size("dp")
+    slot_rows, features = tile_feats.shape
+    nearby = emb_grad.shape[1]
+    most = slot_rows // n
+    width = w_proj.shape[1]
+    q = n // 4
+    shape = (2, 2, q, features // n, width)
+    rounds = (ROUNDS, q)
+    smem = pl.BlockSpec(memory_space=pltpu.SMEM)
+    scratch = [
+        pltpu.VMEM(tile_feats.shape, BF16),
+        pltpu.VMEM(w_proj.shape, BF16),
+        pltpu.VMEM((slot_rows, width), BF16),
+        pltpu.VMEM((n, 1, most), jnp.int32),
+        pltpu.VMEM((n, 1, most), jnp.int32),
+        pltpu.VMEM((2, n, most, width), BF16),
+        pltpu.VMEM((2, nearby, width), BF16),
+        pltpu.VMEM((n, most, width), BF16),
+        pltpu.VMEM((n, most, width), BF16),
+        pltpu.VMEM((D, 4 * width), BF16),
+        pltpu.VMEM((D, width), BF16),
+        pltpu.VMEM((2 * nearby, D), BF16),
+        pltpu.VMEM((3, 2 * nearby, width), BF16),
+        pltpu.VMEM((nearby, width), BF16),
+        pltpu.VMEM((nearby, width), BF16),
+        pltpu.VMEM((nearby, width), BF16),
+        pltpu.VMEM(shape, BF16),
+        pltpu.VMEM(shape[1:], BF16),
+        pltpu.VMEM(shape[2:], BF16),
+        pltpu.VMEM(shape[2:], BF16),
+        pltpu.VMEM(shape[2:], BF16),
+        pltpu.VMEM(shape[2:], BF16),
+        DMA((3,)),
+    ]
+    scratch += [DMA((1,))] * 2
+    scratch += [DMA((n,))] * 8
+    scratch += [DMA((q + 1,))] * 4
+    scratch += [DMA((q,))] * 2
+    scratch += [DMA((2, q))] * 2
+    scratch += [DMA((1,))] * 2
+    scratch += [DMA((width // 128,))] * 2
+    scratch += [DMA((ROUNDS, 2, q))] * 2
+    scratch += [DMA(rounds)] * 8
+    scratch += [DMA((ROUNDS, 2, q))] * 2
+    row = jax.ShapeDtypeStruct((nearby, D), BF16)
+    emb, branch, summed = pl.pallas_call(
+        functools.partial(fused_kernel, n),
+        out_shape=(row, row, jax.ShapeDtypeStruct(shape, BF16)),
+        in_specs=[ANY, VM, smem, ANY, ANY, VM, VM, VM],
+        out_specs=(VM, VM, VM),
+        scratch_shapes=scratch,
+        compiler_params=pltpu.CompilerParams(
+            collective_id=5, has_side_effects=True, vmem_limit_bytes=48 * 1024 * 1024
+        ),
+        cost_estimate=pl.CostEstimate(
+            flops=5_000_000_000, bytes_accessed=10_000_000, transcendentals=1_000_000
+        ),
+    )(tile_feats, tile_pos, slide_count, w_proj, emb_grad, ln_gain, w_qkv, w_out)
+    return (emb[None], branch[None], summed.reshape(features, width).astype(F32))
+
+
 def solution(mesh):
     in_specs = (
         P("dp", None),
@@ -520,4 +1192,6 @@
         P("dp", None),
     )
     out_specs = (P("dp", "seq", None), P("dp", "seq", None), P(None, "seq"))
-    return jax.shard_map(local, mesh=mesh, in_specs=in_specs, out_specs=out_specs, check_vma=False)
+    one_kernel = mesh.shape["dp"] == 16 and mesh.shape["seq"] == 2
+    body = fused if one_kernel else local
+    return jax.shard_map(body, mesh=mesh, in_specs=in_specs, out_specs=out_specs, check_vma=False)

time: 119 us -> 85 us (0.71)
  Pallas kernels: 90 us -> 74.3 us
  between operations: 14.9 us -> 1.3 us
  other arithmetic: 6.53 us -> 2.03 us
  local copies, waits for them, and re-layouts: 2.67 us -> 7.07 us
  matrix products: 4.35 us -> 0 us
    pallas_call x3 -> x1, Pallas kernels: 90 us -> 74.3 us  [fused(): pl.pallas_call(functools.partial(fused_kernel, n), out_shape=(row, row, j...]
    unnamed x8 -> x14, local copies, waits for them, and re-layouts: 1.7 us -> 7.07 us
    dot_general x2 -> x0, matrix products: 4.35 us -> none  [the longest x1 2.84 us: local(): jnp.dot(tile_feats, w_proj, preferred_element_type=F32).astype(BF16)]
    concatenate x1 -> x0, other arithmetic: 1.82 us -> none  [local(): jnp.concatenate([w_qkv, w_out], axis=1)]
    unnamed x1 -> x0, other arithmetic: 1.34 us -> none
  transfers between devices with their start and end apart: 1 -> 0, of which waited for: 0 -> 0; matrix products, arithmetic and copies ran while one was open for 10% -> 0% of each run, Pallas kernels for 66% -> 0%
where the time goes in v1:
time: 85 us; the launch traced here: 84.7 us
  Pallas kernels  74.3 us (87%)
  local copies, waits for them, and re-layouts  7.07 us (8%)
  other arithmetic  2.03 us (2%)
  between operations  1.3 us (2%)
    pallas_call x1, Pallas kernels, fused(): pl.pallas_call(functools.partial(fused_kernel, n), out_shape=(row, row, j...  74.3 us
    unnamed x14, local copies, waits for them, and re-layouts  7.07 us
    convert_element_type x1, other arithmetic, fused(): summed.reshape(features, width).astype(F32)  2.03 us

profile of v1, /device:TPU:0, one launch (start us, length us, event | category | flops | bytes accessed | tf_op | source)
XLA Modules:
  0.0 84.7 jit_solution(13751702373048021602)
XLA Ops:
  1.3 0.0 copy-start
  1.3 1.4 %copy-done = bf16[2048,384]{1,0:T(8,128)(2,1)S(1)} copy-done((bf16[2048,384]{1,0:T(8,128)(2,1)S(1)}, bf16[2048,384]{1,0:T(8,128)(2,1)}, u32[]{:S(2)}) %copy-start) | copy-done | bytes 1572888
  2.7 0.0 copy-start.1
  2.7 1.0 %copy-done.1 = bf16[1,256,768]{2,1,0:T(8,128)(2,1)S(1)} copy-done((bf16[1,256,768]{2,1,0:T(8,128)(2,1)S(1)}, bf16[1,256,768]{2,1,0:T(8,128)(2,1)}, u32[]{:S(2)}) %copy-start.1) | copy-done | bytes 393240
  3.7 0.0 copy-start.2
  3.7 0.9 %copy-done.2 = bf16[48,2304]{1,0:T(8,128)(2,1)S(1)} copy-done((bf16[48,2304]{1,0:T(8,128)(2,1)S(1)}, bf16[48,2304]{1,0:T(8,128)(2,1)}, u32[]{:S(2)}) %copy-start.2) | copy-done | bytes 221208
  4.6 0.0 copy-start.3
  4.6 0.9 %copy-done.3 = bf16[48,768]{1,0:T(8,128)(2,1)S(1)} copy-done((bf16[48,768]{1,0:T(8,128)(2,1)S(1)}, bf16[48,768]{1,0:T(8,128)(2,1)}, u32[]{:S(2)}) %copy-start.3) | copy-done | bytes 73752
  5.5 0.0 copy-start.4
  5.5 0.7 copy-done.4
  6.2 0.0 copy-start.5
  6.2 0.7 copy-done.5
  6.9 74.3 %shard_map.103 = (bf16[256,768]{1,0:T(8,128)(2,1)S(1)}, bf16[256,768]{1,0:T(8,128)(2,1)S(1)}, bf16[2,2,4,128,384]{4,3,2,1,0:T(8,128)(2,1)S(1)}) custom-call(bf16[512,2048]{1,0:T(8,128)(2,1)} %feats_hbm.1, s32[1,512]{1,0:T(1,128)S(1)} %copy-done.5, s32[1]{0:T(128)S(6)} %copy.13.slide_count, bf16[2048,384]{1,0:T(8,128)(2,1)S(1)} %copy-done, ...), custom_call_target="tpu_custom_call" | custom-call | flops 5000000000 | bytes 10000000 | tf_op jit(solution)/shard_map/pallas_call | solution.py:1167
  81.2 2.0 %bitcast_convert_fusion = f32[2048,384]{1,0:T(8,128)} fusion(bf16[2,2,4,128,384]{4,3,2,1,0:T(8,128)(2,1)S(1)} %get-tuple-element.8), kind=kLoop, calls=%fused_computation | loop fusion | flops 786432 | bytes 4718592 | tf_op jit(solution)/shard_map/convert_element_type | solution.py:1180
  83.2 0.7 copy.14
  83.9 0.7 copy.15
Async XLA Ops:
  1.3 1.4 %copy-start = (bf16[2048,384]{1,0:T(8,128)(2,1)S(1)}, bf16[2048,384]{1,0:T(8,128)(2,1)}, u32[]{:S(2)}) copy-start(bf16[2048,384]{1,0:T(8,128)(2,1)} %wproj_hbm.1) | copy-start | bytes 4718596
  2.7 1.0 %copy-start.1 = (bf16[1,256,768]{2,1,0:T(8,128)(2,1)S(1)}, bf16[1,256,768]{2,1,0:T(8,128)(2,1)}, u32[]{:S(2)}) copy-start(bf16[1,256,768]{2,1,0:T(8,128)(2,1)} %grad.1) | copy-start | bytes 1179652
  3.7 0.9 %copy-start.2 = (bf16[48,2304]{1,0:T(8,128)(2,1)S(1)}, bf16[48,2304]{1,0:T(8,128)(2,1)}, u32[]{:S(2)}) copy-start(bf16[48,2304]{1,0:T(8,128)(2,1)} %wqkv.1) | copy-start | bytes 663556
  4.6 0.9 %copy-start.3 = (bf16[48,768]{1,0:T(8,128)(2,1)S(1)}, bf16[48,768]{1,0:T(8,128)(2,1)}, u32[]{:S(2)}) copy-start(bf16[48,768]{1,0:T(8,128)(2,1)} %wout.1) | copy-start | bytes 221188
  5.5 0.7 copy-start.4
  6.2 0.7 copy-start.5

commit v2 on v1

--- a/solution.py
+++ b/solution.py
@@ -509,7 +509,7 @@
 
 
 ROUNDS = 2
-ANY = pl.BlockSpec(memory_space=pl.ANY)
+HBM = pl.BlockSpec(memory_space=pltpu.HBM)
 NT = (((1,), (1,)), ((), ()))
 TN = (((0,), (0,)), ((), ()))
 
@@ -522,18 +522,22 @@
 def fused_kernel(
     n,
     feats_hbm,
-    pos,
+    pos_hbm,
     slide_count,
     wproj_hbm,
     grad,
-    gain,
-    wqkv,
-    wout,
+    gain_hbm,
+    wqkv_hbm,
+    wout_hbm,
     emb_ref,
     branch_ref,
     out,
     feats,
     wproj,
+    pos,
+    gain,
+    wqkv,
+    wout,
     emb,
     pos_in,
     pos_all,
@@ -608,6 +612,14 @@
 
     feats_copy = pltpu.make_async_copy(feats_hbm, feats, local_sems.at[0])
     wproj_copy = pltpu.make_async_copy(wproj_hbm, wproj, local_sems.at[1])
+    pos_load = pltpu.make_async_copy(pos_hbm, pos, local_sems.at[3])
+    gain_load = pltpu.make_async_copy(gain_hbm, gain, local_sems.at[4])
+    wqkv_load = pltpu.make_async_copy(wqkv_hbm, wqkv, local_sems.at[5])
+    wout_load = pltpu.make_async_copy(wout_hbm, wout, local_sems.at[6])
+    pos_load.start()
+    wqkv_load.start()
+    wout_load.start()
+    gain_load.start()
     wproj_copy.start()
     feats_copy.start()
     barrier = pltpu.get_barrier_semaphore()
@@ -618,8 +630,12 @@
 
     pl.semaphore_signal(barrier, device_id=x_peer, device_id_type=MESH)
 
+    pos_load.wait()
     for i in range(n):
         pos_in[i] = pos[:, i * most : (i + 1) * most]
+    wqkv_load.wait()
+    wout_load.wait()
+    gain_load.wait()
     mine_w = pl.ds(pl.multiple_of(dp * depth, 16), depth)
     half = pl.multiple_of(seq * width, width)
     for i in range(3):
@@ -1118,6 +1134,43 @@
     reduce_done()
 
 
+def finish_kernel(emb, branch, summed, emb_out, branch_out, grad_out, wide, sems):
+    copies = [
+        pltpu.make_async_copy(emb, emb_out.at[0], sems.at[0]),
+        pltpu.make_async_copy(branch, branch_out.at[0], sems.at[1]),
+    ]
+    for copy in copies:
+        copy.start()
+    size = summed.shape[0] // 4
+    for i in range(4):
+        at = pl.ds(i * size, size)
+        wide[at, :] = summed[at, :].astype(F32)
+        copies.append(pltpu.make_async_copy(wide.at[at], grad_out.at[at], sems.at[2 + i]))
+        copies[-1].start()
+    for copy in copies:
+        copy.wait()
+
+
+def finish(emb, branch, summed):
+    return pl.pallas_call(
+        finish_kernel,
+        out_shape=(
+            jax.ShapeDtypeStruct((1, *emb.shape), BF16),
+            jax.ShapeDtypeStruct((1, *branch.shape), BF16),
+            jax.ShapeDtypeStruct(summed.shape, F32),
+        ),
+        in_specs=[VM] * 3,
+        out_specs=(HBM,) * 3,
+        scratch_shapes=[pltpu.VMEM(summed.shape, F32), DMA((6,))],
+        compiler_params=pltpu.CompilerParams(vmem_limit_bytes=16 * 1024 * 1024),
+        cost_estimate=pl.CostEstimate(flops=0, bytes_accessed=6_000_000, transcendentals=0),
+    )(emb, branch, summed)
+
+
+def in_hbm(operand):
+    return pltpu.with_memory_space_constraint(operand, pltpu.HBM)
+
+
 def fused(tile_feats, tile_pos, slide_count, w_proj, emb_grad, ln_gain, w_qkv, w_out):
     n = lax.axis_size("dp")
     slot_rows, features = tile_feats.shape
@@ -1131,6 +1184,10 @@
     scratch = [
         pltpu.VMEM(tile_feats.shape, BF16),
         pltpu.VMEM(w_proj.shape, BF16),
+        pltpu.VMEM(tile_pos.shape, jnp.int32),
+        pltpu.VMEM(ln_gain.shape, F32),
+        pltpu.VMEM(w_qkv.shape, BF16),
+        pltpu.VMEM(w_out.shape, BF16),
         pltpu.VMEM((slot_rows, width), BF16),
         pltpu.VMEM((n, 1, most), jnp.int32),
         pltpu.VMEM((n, 1, most), jnp.int32),
@@ -1151,7 +1208,7 @@
         pltpu.VMEM(shape[2:], BF16),
         pltpu.VMEM(shape[2:], BF16),
         pltpu.VMEM(shape[2:], BF16),
-        DMA((3,)),
+        DMA((7,)),
     ]
     scratch += [DMA((1,))] * 2
     scratch += [DMA((n,))] * 8
@@ -1167,7 +1224,7 @@
     emb, branch, summed = pl.pallas_call(
         functools.partial(fused_kernel, n),
         out_shape=(row, row, jax.ShapeDtypeStruct(shape, BF16)),
-        in_specs=[ANY, VM, smem, ANY, ANY, VM, VM, VM],
+        in_specs=[HBM, HBM, smem, HBM, HBM, HBM, HBM, HBM],
         out_specs=(VM, VM, VM),
         scratch_shapes=scratch,
         compiler_params=pltpu.CompilerParams(
@@ -1176,8 +1233,17 @@
         cost_estimate=pl.CostEstimate(
             flops=5_000_000_000, bytes_accessed=10_000_000, transcendentals=1_000_000
         ),
-    )(tile_feats, tile_pos, slide_count, w_proj, emb_grad, ln_gain, w_qkv, w_out)
-    return (emb[None], branch[None], summed.reshape(features, width).astype(F32))
+    )(
+        in_hbm(tile_feats),
+        in_hbm(tile_pos),
+        slide_count,
+        in_hbm(w_proj),
+        in_hbm(emb_grad),
+        in_hbm(ln_gain),
+        in_hbm(w_qkv),
+        in_hbm(w_out),
+    )
+    return finish(emb, branch, summed.reshape(features, width))
 
 
 def solution(mesh):

time: 85 us -> 78.1 us (0.919)
  local copies, waits for them, and re-layouts: 7.07 us -> 0 us
  Pallas kernels: 74.3 us -> 76.6 us
  other arithmetic: 2.03 us -> 0 us
    unnamed x14 -> x0, local copies, waits for them, and re-layouts: 7.07 us -> none
    convert_element_type x1 -> x0, other arithmetic: 2.03 us -> none  [fused(): summed.reshape(features, width).astype(F32)]
    pallas_call x0 -> x1, Pallas kernels: none -> 1.97 us  [finish(): pl.pallas_call(finish_kernel, out_shape=(jax.ShapeDtypeStruct((1, *emb.sh...]
where the time goes in v2:
time: 78.1 us; the launch traced here: 77.9 us
  Pallas kernels  76.6 us (98%)
  between operations  1.29 us (2%)
    pallas_call x1, Pallas kernels, fused(): pl.pallas_call(functools.partial(fused_kernel, n), out_shape=(row, row, j...  74.7 us
    pallas_call x1, Pallas kernels, finish(): pl.pallas_call(finish_kernel, out_shape=(jax.ShapeDtypeStruct((1, *emb.sh...  1.97 us

profile of v2, /device:TPU:0, one launch (start us, length us, event | category | flops | bytes accessed | tf_op | source)
XLA Modules:
  0.0 77.9 jit_solution(9306646490474142634)
XLA Ops:
  1.3 74.7 %shard_map.103 = (bf16[256,768]{1,0:T(8,128)(2,1)S(1)}, bf16[256,768]{1,0:T(8,128)(2,1)S(1)}, bf16[2,2,4,128,384]{4,3,2,1,0:T(8,128)(2,1)S(1)}) custom-call(bf16[512,2048]{1,0:T(8,128)(2,1)} %feats_hbm.1, s32[1,512]{1,0:T(1,128)} %pos_hbm.1, s32[1]{0:T(128)S(6)} %copy.11.slide_count, bf16[2048,384]{1,0:T(8,128)(2,1)} %wproj_hbm.1, ...), custom_call_target="tpu_custom_call" | custom-call | flops 5000000000 | bytes 10000000 | tf_op jit(solution)/shard_map/pallas_call | solution.py:1224
  75.9 2.0 %shard_map.104 = (bf16[1,256,768]{2,1,0:T(8,128)(2,1)}, bf16[1,256,768]{2,1,0:T(8,128)(2,1)}, f32[2048,384]{1,0:T(8,128)}) custom-call(bf16[256,768]{1,0:T(8,128)(2,1)S(1)} %get-tuple-element.6.emb, bf16[256,768]{1,0:T(8,128)(2,1)S(1)} %get-tuple-element.7.branch, bf16[2048,384]{1,0:T(8,128)(2,1)S(1)} %bitcast.1), custom_call_target="tpu_custom_call" | custom-call | bytes 6000000 | tf_op jit(solution)/shard_map/pallas_call | solution.py:1155

commit v3 on v2

--- a/solution.py
+++ b/solution.py
@@ -508,15 +508,10 @@
     return (local_emb[None], attn_branch[None], proj_grad)
 
 
-ROUNDS = 2
+SPLIT = 5
 HBM = pl.BlockSpec(memory_space=pltpu.HBM)
 NT = (((1,), (1,)), ((), ()))
 TN = (((0,), (0,)), ((), ()))
-
-
-def split_first(count):
-    size = count // ROUNDS
-    return [pl.ds(r * size, size) for r in range(ROUNDS)]
 
 
 def fused_kernel(
@@ -555,9 +550,13 @@
     src,
     pair,
     cross,
-    stage_b,
-    stage_c,
-    arrive,
+    stage_y,
+    stage_za,
+    stage_zb,
+    in_za,
+    in_zb,
+    stage_yb,
+    cross_b,
     local_sems,
     xs,
     xr,
@@ -589,10 +588,18 @@
     r3,
     s4,
     r4,
-    s5,
-    r5,
-    s6,
-    r6,
+    gus,
+    gur,
+    gds,
+    gdr,
+    gys,
+    gyr,
+    gbs,
+    gbr,
+    gcs,
+    gcr,
+    gxs,
+    gxr,
 ):
     dp, seq = lax.axis_index("dp"), lax.axis_index("seq")
     q = n // 4
@@ -610,6 +617,13 @@
     inner = HEAD_COUNT * HEAD_WIDTH
     wide = 3 * width
 
+    barrier = pltpu.get_barrier_semaphore()
+
+    @pl.loop(1, n)
+    def _(t):
+        pl.semaphore_signal(barrier, device_id=(lax.rem(dp + t, n), seq), device_id_type=MESH)
+
+    pl.semaphore_signal(barrier, device_id=x_peer, device_id_type=MESH)
     feats_copy = pltpu.make_async_copy(feats_hbm, feats, local_sems.at[0])
     wproj_copy = pltpu.make_async_copy(wproj_hbm, wproj, local_sems.at[1])
     pos_load = pltpu.make_async_copy(pos_hbm, pos, local_sems.at[3])
@@ -622,14 +636,6 @@
     gain_load.start()
     wproj_copy.start()
     feats_copy.start()
-    barrier = pltpu.get_barrier_semaphore()
-
-    @pl.loop(1, n)
-    def _(t):
-        pl.semaphore_signal(barrier, device_id=(lax.rem(dp + t, n), seq), device_id_type=MESH)
-
-    pl.semaphore_signal(barrier, device_id=x_peer, device_id_type=MESH)
-
     pos_load.wait()
     for i in range(n):
         pos_in[i] = pos[:, i * most : (i + 1) * most]
@@ -678,51 +684,6 @@
     def grad_recv(source):
         return remote(picked.at[source], slots.at[source], gs.at[source], gr.at[source], sibling)
 
-    pl.semaphore_wait(barrier, n)
-    column_copy().start()
-
-    @pl.loop(1, n)
-    def _(t):
-        pos_copy(t).start()
-
-    wproj_copy.wait()
-    feats_copy.wait()
-    emb[...] = jnp.dot(feats[...], wproj[...], preferred_element_type=F32).astype(BF16)
-
-    @pl.loop(1, n)
-    def _(t):
-        emb_copy(t).start()
-
-    emb_all[seq, dp] = emb[pl.ds(pl.multiple_of(dp * most, most), most), :]
-    forward(0).start()
-
-    @pl.loop(1, n)
-    def _(t):
-        pos_copy(t).wait()
-
-    own_columns.wait()
-    column_copy().wait()
-    rows = jnp.concatenate([grad_rows[0], grad_rows[1]], axis=0)
-    spot = lax.broadcasted_iota(jnp.int32, (2 * nearby, 1), 0)
-    batch = 4
-
-    @pl.loop(1, q + 1)
-    def _(step):
-        first = lax.rem(c + step, q) * batch
-        at = jnp.concatenate([pos_all[first + i] for i in range(batch)], axis=1)
-        hot = jnp.where(spot == at, 1.0, 0.0).astype(BF16)
-        block = lax.dot_general(hot, rows, TN, preferred_element_type=F32).astype(BF16)
-        for i in range(batch):
-            picked[first + i] = block[i * most : (i + 1) * most]
-
-            @pl.when(first + i != dp)
-            def _():
-                grad_send(first + i).start()
-
-            @pl.when(first + i == dp)
-            def _():
-                slots[first + i] = block[i * most : (i + 1) * most]
-
     def rows_of(who):
         return pl.ds(pl.multiple_of(who * depth, 16), depth)
 
@@ -820,35 +781,90 @@
 
         wx_copy().wait_send()
 
-    w_start()
-
-    @pl.loop(1, n)
-    def _(t):
-        emb_copy(t).wait_recv()
-        forward(t).start()
-
-    w_hop(1)
-    w_hop(2)
-
-    count = slide_count[0]
+    spot = lax.broadcasted_iota(jnp.int32, (2 * nearby, 1), 0)
+
+    @pl.when(c == 0)
+    def _():
+        in_za[0] = jnp.zeros_like(in_za[0])
+        in_zb[0] = jnp.zeros_like(in_zb[0])
+
+    @pl.when(c == q - 1)
+    def _():
+        in_za[1] = jnp.zeros_like(in_za[1])
+        in_zb[1] = jnp.zeros_like(in_zb[1])
+
+    def first_sends():
+        pl.semaphore_wait(barrier, n)
+        column_copy().start()
+
+        @pl.loop(1, n)
+        def _(t):
+            pos_copy(t).start()
+
+    def embed():
+        wproj_copy.wait()
+        feats_copy.wait()
+        emb[...] = jnp.dot(feats[...], wproj[...], preferred_element_type=F32).astype(BF16)
+
+    def emb_sends():
+        @pl.loop(1, n)
+        def _(t):
+            emb_copy(t).start()
+
+        emb_all[seq, dp] = emb[pl.ds(pl.multiple_of(dp * most, most), most), :]
+        forward(0).start()
+
+    def emb_on(low, high):
+        @pl.loop(low, high)
+        def _(t):
+            emb_copy(t).wait_recv()
+            forward(t).start()
+
+    def grad_sends():
+        @pl.loop(1, n)
+        def _(t):
+            pos_copy(t).wait()
+
+        own_columns.wait()
+        column_copy().wait()
+        rows = jnp.concatenate([grad_rows[0], grad_rows[1]], axis=0)
+        batch = 4
+
+        @pl.loop(1, q + 1)
+        def _(step):
+            first = lax.rem(c + step, q) * batch
+            at = jnp.concatenate([pos_all[first + i] for i in range(batch)], axis=1)
+            hot = jnp.where(spot == at, 1.0, 0.0).astype(BF16)
+            block = lax.dot_general(hot, rows, TN, preferred_element_type=F32).astype(BF16)
+            for i in range(batch):
+                picked[first + i] = block[i * most : (i + 1) * most]
+
+                @pl.when(first + i != dp)
+                def _():
+                    grad_send(first + i).start()
+
+                @pl.when(first + i == dp)
+                def _():
+                    slots[first + i] = block[i * most : (i + 1) * most]
+
+    count = slide_count[:, 0:1]
     own = pl.multiple_of(seq * nearby, nearby)
     far_own = pl.multiple_of((1 - seq) * nearby, nearby)
-    positions = jnp.concatenate([pos_all[i] for i in range(n)], axis=1)
 
     def natural_of(index, shift):
         return (index % part) * DILATION_STEP + lax.rem(index // part + 2 * shift, DILATION_STEP)
 
-    inside = spot % nearby
-    at_spot = spot - inside + natural_of(inside, seq)
-    hot_perm = jnp.where(at_spot == positions, 1.0, 0.0).astype(BF16)
-    own_spot = lax.broadcasted_iota(jnp.int32, (nearby, 1), 0) + seq * nearby
-    hot_own = jnp.where(own_spot == positions, 1.0, 0.0).astype(BF16)
-
-    @pl.loop(0, n)
-    def _(t):
-        forward(t).wait_recv()
-
     def regroup():
+        @pl.loop(0, n)
+        def _(t):
+            forward(t).wait_recv()
+
+        positions = jnp.concatenate([pos_all[i] for i in range(n)], axis=1)
+        inside = spot % nearby
+        at_spot = spot - inside + natural_of(inside, seq)
+        hot_perm = jnp.where(at_spot == positions, 1.0, 0.0).astype(BF16)
+        own_spot = lax.broadcasted_iota(jnp.int32, (nearby, 1), 0) + seq * nearby
+        hot_own = jnp.where(own_spot == positions, 1.0, 0.0).astype(BF16)
         blocks = [emb_all[i].reshape(slot_rows, width) for i in range(2)]
         for i in range(2):
             emb_ref[:, i * width : (i + 1) * width] = jnp.dot(
@@ -866,139 +882,258 @@
                 (row - center) * lax.rsqrt(spread + EPSILON) * gain[...][None, :]
             ).astype(BF16)
 
-    regroup()
-
-    ranges = split_first(src.shape[3])
-
-    def side(i):
-        return 1 - b if i == 0 else b
-
-    def ahead(t):
-        return lax.rem(c + t, q)
-
-    def behind(t):
-        return lax.rem(c - t + q, q)
-
-    def along(t):
-        return (ahead(t) * 4 + b * 2 + a, seq)
-
-    def to_sibling(r, i, t):
-        at = ranges[r]
+    rows_each = src.shape[3]
+    cut = rows_each * SPLIT // 8
+    at_a, at_b = pl.ds(0, cut), pl.ds(cut, rows_each - cut)
+    both = pl.ds(0, 2)
+
+    def to_sibling(part, y, k):
+        at = (at_a, at_b)[part]
         return remote(
-            src.at[1 - a, side(i), ahead(t), at],
-            pair.at[i, t, at],
-            s1.at[r, i, t],
-            r1.at[r, i, t],
+            src.at[1 - a, y, k, at],
+            pair.at[y, k, at],
+            s1.at[part, y, k],
+            r1.at[part, y, k],
             sibling,
         )
 
-    def to_across(r, t):
-        at = ranges[r]
-        return remote(stage_b.at[t, at], cross.at[t, at], s2.at[r, t], r2.at[r, t], across)
-
-    def to_owner(r, t):
-        at = ranges[r]
-        return remote(stage_c.at[t, at], arrive.at[t, at], s3.at[r, t], r3.at[r, t], along(t))
-
-    def result_along(r, t):
-        block = out.at[a, b, c, ranges[r]]
-        return remote(block, block, s4.at[r, t], r4.at[r, t], along(t))
-
-    def result_across(r, t):
-        block = out.at[a, b, behind(t), ranges[r]]
-        return remote(block, block, s5.at[r, t], r5.at[r, t], across)
-
-    def result_sibling(r, i, t):
-        block = out.at[a, side(i), behind(t), ranges[r]]
-        return remote(block, block, s6.at[r, i, t], r6.at[r, i, t], sibling)
-
-    order = [t % q for t in range(1, q + 1)]
-
-    @pl.loop(0, n)
-    def _(source):
-        @pl.when(source != dp)
+    def turn(j):
+        return lax.select(c < q // 2, q - 1 - j, j)
+
+    def send_pairs(y):
+        for part in range(2):
+            for j in range(q):
+                to_sibling(part, y, turn(j)).start()
+
+    def to_across(k):
+        return remote(stage_y.at[k], cross.at[k], s2.at[k], r2.at[k], across)
+
+    def to_z(part, d, k):
+        stage, land = ((stage_za, in_za), (stage_zb, in_zb))[part]
+        peer = lax.rem(dp + n + 4 - 8 * d, n)
+        return remote(stage.at[k], land.at[d, k], s3.at[part, k], r3.at[part, d, k], (peer, seq))
+
+    def to_across_b():
+        return remote(stage_yb, cross_b, s4.at[0], r4.at[0], across)
+
+    def block_of(part, k):
+        return out.at[a, b, k, at_a] if part == 0 else out.at[a, both, k, at_b]
+
+    def go_up(part, hop, k):
+        block = block_of(part, k)
+        device = (lax.rem(dp + 4, n), seq)
+        return remote(block, block, gus.at[part, hop], gur.at[part, hop], device)
+
+    def go_down(part, hop, k):
+        block = block_of(part, k)
+        device = (lax.rem(dp + n - 4, n), seq)
+        return remote(block, block, gds.at[part, hop], gdr.at[part, hop], device)
+
+    def go_across(k):
+        block = out.at[a, b, k, at_a]
+        return remote(block, block, gys.at[k], gyr.at[k], across)
+
+    def go_across_b():
+        block = out.at[a, b, c, at_b]
+        return remote(block, block, gbs.at[0], gbr.at[0], across)
+
+    def go_sibling(side, k):
+        block = out.at[a, b if side == 0 else 1 - b, k, at_a]
+        return remote(block, block, gcs.at[side, k], gcr.at[side, k], sibling)
+
+    def go_sibling_b(k):
+        block = out.at[a, both, k, at_b]
+        return remote(block, block, gxs.at[k], gxr.at[k], sibling)
+
+    def product():
+        @pl.loop(0, n)
+        def _(source):
+            @pl.when(source != dp)
+            def _():
+                grad_recv(source).wait_recv()
+
+        grads = slots[...].reshape(slot_rows, width)
+        tile = q * rows_each
+
+        @pl.loop(0, n // q)
+        def _(step):
+            core = lax.rem(1 - a + step // 2, 2)
+            y = lax.rem(1 - b + step, 2)
+            first = pl.multiple_of((core * 2 + y) * tile, tile)
+            product = lax.dot_general(
+                feats[:, pl.ds(first, tile)], grads, TN, preferred_element_type=F32
+            ).astype(BF16)
+            for i in range(q):
+                src[core, y, i] = product[i * rows_each : (i + 1) * rows_each]
+
+            @pl.when(step < 2)
+            def _():
+                send_pairs(y)
+
+    def sum_y(j):
+        k = turn(j)
+        to_sibling(0, 1 - b, k).wait_recv()
+        stage_y[k] = (
+            src[a, 1 - b, k, at_a].astype(F32) + pair[1 - b, k, at_a].astype(F32)
+        ).astype(BF16)
+        to_across(k).start()
+
+    def term_a(k):
+        return (
+            src[a, b, k, at_a].astype(F32)
+            + pair[b, k, at_a].astype(F32)
+            + cross[k].astype(F32)
+        )
+
+    def term_b(k):
+        return src[a, both, k, at_b].astype(F32) + pair[both, k, at_b].astype(F32)
+
+    def ready(part, k):
+        if part == 0:
+            to_sibling(0, b, k).wait_recv()
+            to_across(k).wait_recv()
+        else:
+            to_sibling(1, 0, k).wait_recv()
+            to_sibling(1, 1, k).wait_recv()
+
+    def sum_z(part, j):
+        k = turn(j)
+        term, stage, land = ((term_a, stage_za, in_za), (term_b, stage_zb, in_zb))[part]
+        ready(part, k)
+
+        @pl.when(k > c)
         def _():
-            grad_recv(source).wait_recv()
-
-    rows_each = src.shape[3]
-    grads = slots[...].reshape(slot_rows, width)
-    tile = q * rows_each
-
-    @pl.loop(0, n // q)
-    def _(step):
-        core = lax.rem(1 - a + step // 2, 2)
-        y = lax.rem(1 - b + step, 2)
-        first = pl.multiple_of((core * 2 + y) * tile, tile)
-        product = lax.dot_general(
-            feats[:, pl.ds(first, tile)], grads, TN, preferred_element_type=F32
+            @pl.when(c > 0)
+            def _():
+                to_z(part, 0, k).wait_recv()
+
+            stage[k] = (term(k) + land[0, k].astype(F32)).astype(BF16)
+            to_z(part, 0, k).start()
+
+        @pl.when(k < c)
+        def _():
+            @pl.when(c < q - 1)
+            def _():
+                to_z(part, 1, k).wait_recv()
+
+            stage[k] = (term(k) + land[1, k].astype(F32)).astype(BF16)
+            to_z(part, 1, k).start()
+
+    def own_in(part):
+        @pl.when(c > 0)
+        def _():
+            to_z(part, 0, c).wait_recv()
+
+        @pl.when(c < q - 1)
+        def _():
+            to_z(part, 1, c).wait_recv()
+
+    def hand_on(part, k):
+        if part == 0:
+            go_across(k).start()
+            go_sibling(0, k).start()
+        else:
+            go_sibling_b(k).start()
+
+    def share(part):
+        @pl.when(c < q - 1)
+        def _():
+            go_up(part, 1, c).start()
+
+        @pl.when(c > 0)
+        def _():
+            go_down(part, 1, c).start()
+
+        hand_on(part, c)
+
+    def own_a():
+        own_in(0)
+        out[a, b, c, at_a] = (
+            term_a(c) + in_za[0, c].astype(F32) + in_za[1, c].astype(F32)
         ).astype(BF16)
-        for i in range(q):
-            src[core, y, i] = product[i * rows_each : (i + 1) * rows_each]
-
-        for i in range(2):
-
-            @pl.when(step == i)
+        share(0)
+
+    def own_b():
+        own_in(1)
+        stage_yb[...] = (
+            src[a, 1 - b, c, at_b].astype(F32)
+            + pair[1 - b, c, at_b].astype(F32)
+            + in_zb[0, c, 1 - b].astype(F32)
+            + in_zb[1, c, 1 - b].astype(F32)
+        ).astype(BF16)
+        to_across_b().start()
+
+    def whole_b():
+        to_across_b().wait_recv()
+        out[a, b, c, at_b] = (
+            src[a, b, c, at_b].astype(F32)
+            + pair[b, c, at_b].astype(F32)
+            + in_zb[0, c, b].astype(F32)
+            + in_zb[1, c, b].astype(F32)
+            + cross_b[...].astype(F32)
+        ).astype(BF16)
+        go_across_b().start()
+
+    def share_b():
+        go_across_b().wait_recv()
+        share(1)
+
+    def result_hop(part, hop):
+        below, above = c - hop, c + hop
+
+        @pl.when(below >= 0)
+        def _():
+            go_up(part, hop, below).wait_recv()
+
+            @pl.when(c < q - 1)
             def _():
-                for r in range(ROUNDS):
-                    for t in order:
-                        to_sibling(r, i, t).start()
-
-    def sum_b(r, t):
-        to_sibling(r, 0, t).wait_recv()
-        at = ranges[r]
-        stage_b[t, at] = (
-            src[a, 1 - b, ahead(t), at].astype(F32) + pair[0, t, at].astype(F32)
-        ).astype(BF16)
-        to_across(r, t).start()
-
-    def sum_c(r, t):
-        to_sibling(r, 1, t).wait_recv()
-        to_across(r, t).wait_recv()
-        at = ranges[r]
-        stage_c[t, at] = (
-            src[a, b, ahead(t), at].astype(F32)
-            + pair[1, t, at].astype(F32)
-            + cross[t, at].astype(F32)
-        ).astype(BF16)
-        if t:
-            to_owner(r, t).start()
-
-    def own_sum(r):
-        at = ranges[r]
-        total = stage_c[0, at].astype(F32)
-        for t in range(1, q):
-            to_owner(r, t).wait_recv()
-            total = total + arrive[t, at].astype(F32)
-        out[a, b, c, at] = total.astype(BF16)
-        for t in range(1, q):
-            result_along(r, t).start()
-        result_across(r, 0).start()
-        result_sibling(r, 1, 0).start()
-
-    def result_on(r, t):
-        result_along(r, t).wait_recv()
-        result_across(r, t).start()
-        result_sibling(r, 1, t).start()
-
-    def result_over(r, t):
-        result_across(r, t).wait_recv()
-        result_sibling(r, 0, t).start()
+                go_up(part, hop + 1, below).start()
+
+            hand_on(part, below)
+
+        @pl.when(above < q)
+        def _():
+            go_down(part, hop, above).wait_recv()
+
+            @pl.when(c > 0)
+            def _():
+                go_down(part, hop + 1, above).start()
+
+            hand_on(part, above)
+
+    def result_over(j):
+        k = lax.rem(c + j, q)
+        go_across(k).wait_recv()
+        go_sibling(1, k).start()
 
     def reduce_done():
-        for r in range(ROUNDS):
-
-            @pl.loop(0, q)
-            def _(t):
-                for i in range(2):
-                    to_sibling(r, i, t).wait_send()
-                    result_sibling(r, i, t).wait()
-                to_across(r, t).wait_send()
-                result_across(r, t).wait_send()
-
-            @pl.loop(1, q)
-            def _(t):
-                to_owner(r, t).wait_send()
-                result_along(r, t).wait_send()
+        @pl.loop(0, q)
+        def _(k):
+            for y in range(2):
+                for part in range(2):
+                    to_sibling(part, y, k).wait_send()
+                go_sibling(y, k).wait()
+            to_across(k).wait_send()
+            go_across(k).wait_send()
+            go_sibling_b(k).wait()
+
+            @pl.when(k != c)
+            def _():
+                for part in range(2):
+                    to_z(part, 0, k).wait_send()
+
+        to_across_b().wait_send()
+        go_across_b().wait_send()
+        for part in range(2):
+            for hop in range(1, q):
+
+                @pl.when((c - hop + 1 >= 0) & (c < q - 1))
+                def _():
+                    go_up(part, hop, c - hop + 1).wait_send()
+
+                @pl.when((c + hop - 1 < q) & (c > 0))
+                def _():
+                    go_down(part, hop, c + hop - 1).wait_send()
 
     lane = lax.broadcasted_iota(jnp.int32, (1, nearby), 1)
     row_at = lax.broadcasted_iota(jnp.int32, (nearby, 1), 0)
@@ -1080,42 +1215,36 @@
                 total = term if total is None else total + term
             branch_ref[:, pl.ds(pl.multiple_of(cols * width, width), width)] = total.astype(BF16)
 
-    reduce_steps = []
-    for r in range(ROUNDS):
-        reduce_steps += [functools.partial(sum_b, r, t) for t in order]
-    for r in range(ROUNDS):
-        reduce_steps += [functools.partial(sum_c, r, t) for t in order]
-        reduce_steps += [functools.partial(own_sum, r)]
-        if r:
-            reduce_steps += [functools.partial(result_on, r - 1, t) for t in range(1, q)]
-            reduce_steps += [functools.partial(result_over, r - 1, t) for t in range(q)]
-    r = ROUNDS - 1
-    reduce_steps += [functools.partial(result_on, r, t) for t in range(1, q)]
-    reduce_steps += [functools.partial(result_over, r, t) for t in range(q)]
-
-    work = [functools.partial(project, i) for i in range(3)]
-    work += [functools.partial(heads, False, j) for j in range(pairs)]
-    work += [functools.partial(heads, True, j) for j in range(pairs)]
-
-    w_hop(3)
-    split = 2 * q
-    for step in reduce_steps[:q]:
-        step()
-    w_side()
-    for step in reduce_steps[q:split]:
-        step()
-    w_gathered()
-    rest = reduce_steps[split:]
-    slots_left = len(work)
-    taken = 0
-    for i, job in enumerate(work):
-        job()
-        until = (i + 1) * len(rest) // (slots_left + 2)
-        for step in rest[taken:until]:
-            step()
-        taken = until
-    finish_branch()
-    for step in rest[taken:]:
+    do = functools.partial
+
+    sums = [do(sum_y, 0), do(sum_y, 1), do(sum_z, 1, 0), do(sum_y, 2), do(sum_y, 3)]
+    for j in range(1, q):
+        sums += [do(sum_z, 1, j), do(sum_z, 0, j - 1)]
+    sums += [own_b, do(sum_z, 0, q - 1), whole_b, own_a, share_b]
+    for hop in range(1, q):
+        sums += [do(result_hop, 0, hop), do(result_hop, 1, hop)]
+    sums += [do(result_over, j) for j in range(q)]
+
+    def merge(jobs, others, tail=2):
+        mixed, taken = [], 0
+        for i, job in enumerate(jobs):
+            until = (i + 1) * len(others) // (len(jobs) + tail)
+            mixed += [job] + others[taken:until]
+            taken = until
+        return mixed + others[taken:]
+    steps = [first_sends, embed, emb_sends, grad_sends, w_start, do(emb_on, 1, n), regroup, do(w_hop, 1), product]
+    steps += sums[0:5] + [do(w_hop, 2)]
+    steps += sums[5:8] + [do(w_hop, 3)]
+    steps += sums[8:10] + [w_side]
+    sums = sums[10:]
+    work = [w_gathered]
+    work += [do(project, i) for i in range(3)]
+    work += [do(heads, False, j) for j in range(pairs)]
+    work += [do(heads, True, j) for j in range(pairs)]
+    work += [finish_branch]
+
+    steps += merge(work, sums, 2)
+    for step in steps:
         step()
 
     @pl.loop(1, n)
@@ -1179,8 +1308,9 @@
     width = w_proj.shape[1]
     q = n // 4
     shape = (2, 2, q, features // n, width)
-    rounds = (ROUNDS, q)
-    smem = pl.BlockSpec(memory_space=pltpu.SMEM)
+    cut = features // n * SPLIT // 8
+    part_a = (q, cut, width)
+    part_b = (q, 2, features // n - cut, width)
     scratch = [
         pltpu.VMEM(tile_feats.shape, BF16),
         pltpu.VMEM(w_proj.shape, BF16),
@@ -1204,10 +1334,14 @@
         pltpu.VMEM((nearby, width), BF16),
         pltpu.VMEM(shape, BF16),
         pltpu.VMEM(shape[1:], BF16),
-        pltpu.VMEM(shape[2:], BF16),
-        pltpu.VMEM(shape[2:], BF16),
-        pltpu.VMEM(shape[2:], BF16),
-        pltpu.VMEM(shape[2:], BF16),
+        pltpu.VMEM(part_a, BF16),
+        pltpu.VMEM(part_a, BF16),
+        pltpu.VMEM(part_a, BF16),
+        pltpu.VMEM(part_b, BF16),
+        pltpu.VMEM((2, *part_a), BF16),
+        pltpu.VMEM((2, *part_b), BF16),
+        pltpu.VMEM(part_b[2:], BF16),
+        pltpu.VMEM(part_b[2:], BF16),
         DMA((7,)),
     ]
     scratch += [DMA((1,))] * 2
@@ -1217,14 +1351,20 @@
     scratch += [DMA((2, q))] * 2
     scratch += [DMA((1,))] * 2
     scratch += [DMA((width // 128,))] * 2
-    scratch += [DMA((ROUNDS, 2, q))] * 2
-    scratch += [DMA(rounds)] * 8
-    scratch += [DMA((ROUNDS, 2, q))] * 2
+    scratch += [DMA((2, 2, q))] * 2
+    scratch += [DMA((q,))] * 2
+    scratch += [DMA((2, q)), DMA((2, 2, q))]
+    scratch += [DMA((1,))] * 2
+    scratch += [DMA((2, q + 1))] * 4
+    scratch += [DMA((q,))] * 2
+    scratch += [DMA((1,))] * 2
+    scratch += [DMA((2, q))] * 2
+    scratch += [DMA((q,))] * 2
     row = jax.ShapeDtypeStruct((nearby, D), BF16)
     emb, branch, summed = pl.pallas_call(
         functools.partial(fused_kernel, n),
         out_shape=(row, row, jax.ShapeDtypeStruct(shape, BF16)),
-        in_specs=[HBM, HBM, smem, HBM, HBM, HBM, HBM, HBM],
+        in_specs=[HBM, HBM, VM, HBM, HBM, HBM, HBM, HBM],
         out_specs=(VM, VM, VM),
         scratch_shapes=scratch,
         compiler_params=pltpu.CompilerParams(
@@ -1236,7 +1376,7 @@
     )(
         in_hbm(tile_feats),
         in_hbm(tile_pos),
-        slide_count,
+        jnp.broadcast_to(slide_count[:, None], (1, 128)),
         in_hbm(w_proj),
         in_hbm(emb_grad),
         in_hbm(ln_gain),

time: 78.1 us -> 71.2 us (0.912)
  Pallas kernels: 76.6 us -> 69.8 us
    pallas_call x1, Pallas kernels: 74.7 us -> 67.8 us  [fused(): pl.pallas_call(functools.partial(fused_kernel, n), out_shape=(row, row, j...]
where the time goes in v3:
time: 71.2 us; the launch traced here: 71 us
  Pallas kernels  69.8 us (98%)
  between operations  1.29 us (2%)
    pallas_call x1, Pallas kernels, fused(): pl.pallas_call(functools.partial(fused_kernel, n), out_shape=(row, row, j...  67.8 us
    pallas_call x1, Pallas kernels, finish(): pl.pallas_call(finish_kernel, out_shape=(jax.ShapeDtypeStruct((1, *emb.sh...  1.97 us

profile of v3, /device:TPU:0, one launch (start us, length us, event | category | flops | bytes accessed | tf_op | source)
XLA Modules:
  0.0 71.0 jit_solution(16771751338447233352)
XLA Ops:
  1.3 67.8 %shard_map.103 = (bf16[256,768]{1,0:T(8,128)(2,1)S(1)}, bf16[256,768]{1,0:T(8,128)(2,1)S(1)}, bf16[2,2,4,128,384]{4,3,2,1,0:T(8,128)(2,1)S(1)}) custom-call(bf16[512,2048]{1,0:T(8,128)(2,1)} %feats_hbm.1, s32[1,512]{1,0:T(1,128)} %pos_hbm.1, s32[1,128]{1,0:T(1,128)S(1)} %broadcast_in_dim.9.slide_count, bf16[2048,384]{1,0:T(8,128)(2,1)} %wproj_hbm.1, ...), custom_call_target="tpu_custom_call" | custom-call | flops 5000000000 | bytes 10000000 | tf_op jit(solution)/shard_map/pallas_call | solution.py:1364
  69.1 2.0 %shard_map.104 = (bf16[1,256,768]{2,1,0:T(8,128)(2,1)}, bf16[1,256,768]{2,1,0:T(8,128)(2,1)}, f32[2048,384]{1,0:T(8,128)}) custom-call(bf16[256,768]{1,0:T(8,128)(2,1)S(1)} %get-tuple-element.6.emb, bf16[256,768]{1,0:T(8,128)(2,1)S(1)} %get-tuple-element.7.branch, bf16[2048,384]{1,0:T(8,128)(2,1)S(1)} %bitcast.3), custom_call_target="tpu_custom_call" | custom-call | bytes 6000000 | tf_op jit(solution)/shard_map/pallas_call | solution.py:1284
  (1 shorter events, 0.0 us)

commit v4 on v3

--- a/solution.py
+++ b/solution.py
@@ -804,13 +804,25 @@
     def embed():
         wproj_copy.wait()
         feats_copy.wait()
-        emb[...] = jnp.dot(feats[...], wproj[...], preferred_element_type=F32).astype(BF16)
+        group = n // 2
+
+        @pl.loop(0, 2)
+        def _(step):
+            which = lax.rem(c * 2 // q + 1 + step, 2)
+            at = pl.ds(pl.multiple_of(which * group * most, group * most), group * most)
+            emb[at, :] = jnp.dot(feats[at, :], wproj[...], preferred_element_type=F32).astype(
+                BF16
+            )
+
+            @pl.loop(0, group)
+            def _(i):
+                t = lax.rem(which * group + i - dp + n, n)
+
+                @pl.when(t > 0)
+                def _():
+                    emb_copy(t).start()
 
     def emb_sends():
-        @pl.loop(1, n)
-        def _(t):
-            emb_copy(t).start()
-
         emb_all[seq, dp] = emb[pl.ds(pl.multiple_of(dp * most, most), most), :]
         forward(0).start()
 

time: 71.2 us -> 70.8 us (level)
  no operation moved by 1% of the time
where the time goes in v4:
time: 70.8 us; the launch traced here: 70.6 us
  Pallas kernels  69.3 us (98%)
  between operations  1.29 us (2%)
    pallas_call x1, Pallas kernels, fused(): pl.pallas_call(functools.partial(fused_kernel, n), out_shape=(row, row, j...  67.3 us
    pallas_call x1, Pallas kernels, finish(): pl.pallas_call(finish_kernel, out_shape=(jax.ShapeDtypeStruct((1, *emb.sh...  1.97 us

profile of v4, /device:TPU:0, one launch (start us, length us, event | category | flops | bytes accessed | tf_op | source)
XLA Modules:
  0.0 70.6 jit_solution(9352432996583935399)
XLA Ops:
  1.3 67.3 %shard_map.103 = (bf16[256,768]{1,0:T(8,128)(2,1)S(1)}, bf16[256,768]{1,0:T(8,128)(2,1)S(1)}, bf16[2,2,4,128,384]{4,3,2,1,0:T(8,128)(2,1)S(1)}) custom-call(bf16[512,2048]{1,0:T(8,128)(2,1)} %feats_hbm.1, s32[1,512]{1,0:T(1,128)} %pos_hbm.1, s32[1,128]{1,0:T(1,128)S(1)} %broadcast_in_dim.9.slide_count, bf16[2048,384]{1,0:T(8,128)(2,1)} %wproj_hbm.1, ...), custom_call_target="tpu_custom_call" | custom-call | flops 5000000000 | bytes 10000000 | tf_op jit(solution)/shard_map/pallas_call | solution.py:1376
  68.6 2.0 %shard_map.104 = (bf16[1,256,768]{2,1,0:T(8,128)(2,1)}, bf16[1,256,768]{2,1,0:T(8,128)(2,1)}, f32[2048,384]{1,0:T(8,128)}) custom-call(bf16[256,768]{1,0:T(8,128)(2,1)S(1)} %get-tuple-element.6.emb, bf16[256,768]{1,0:T(8,128)(2,1)S(1)} %get-tuple-element.7.branch, bf16[2048,384]{1,0:T(8,128)(2,1)S(1)} %bitcast.3), custom_call_target="tpu_custom_call" | custom-call | bytes 6000000 | tf_op jit(solution)/shard_map/pallas_call | solution.py:1296
  (1 shorter events, 0.0 us)

commit v5 on v4

--- a/solution.py
+++ b/solution.py
@@ -624,7 +624,12 @@
         pl.semaphore_signal(barrier, device_id=(lax.rem(dp + t, n), seq), device_id_type=MESH)
 
     pl.semaphore_signal(barrier, device_id=x_peer, device_id_type=MESH)
-    feats_copy = pltpu.make_async_copy(feats_hbm, feats, local_sems.at[0])
+    def feats_copy(step):
+        which = lax.rem(c * 2 // q + 1 + step, 2)
+        half_rows = slot_rows // 2
+        at = pl.ds(pl.multiple_of(which * half_rows, half_rows), half_rows)
+        return pltpu.make_async_copy(feats_hbm.at[at], feats.at[at], local_sems.at[7 + step])
+
     wproj_copy = pltpu.make_async_copy(wproj_hbm, wproj, local_sems.at[1])
     pos_load = pltpu.make_async_copy(pos_hbm, pos, local_sems.at[3])
     gain_load = pltpu.make_async_copy(gain_hbm, gain, local_sems.at[4])
@@ -635,7 +640,8 @@
     wout_load.start()
     gain_load.start()
     wproj_copy.start()
-    feats_copy.start()
+    feats_copy(0).start()
+    feats_copy(1).start()
     pos_load.wait()
     for i in range(n):
         pos_in[i] = pos[:, i * most : (i + 1) * most]
@@ -803,11 +809,11 @@
 
     def embed():
         wproj_copy.wait()
-        feats_copy.wait()
         group = n // 2
 
         @pl.loop(0, 2)
         def _(step):
+            feats_copy(step).wait()
             which = lax.rem(c * 2 // q + 1 + step, 2)
             at = pl.ds(pl.multiple_of(which * group * most, group * most), group * most)
             emb[at, :] = jnp.dot(feats[at, :], wproj[...], preferred_element_type=F32).astype(
@@ -844,7 +850,7 @@
 
         @pl.loop(1, q + 1)
         def _(step):
-            first = lax.rem(c + step, q) * batch
+            first = lax.rem(c + step - 1, q) * batch
             at = jnp.concatenate([pos_all[first + i] for i in range(batch)], axis=1)
             hot = jnp.where(spot == at, 1.0, 0.0).astype(BF16)
             block = lax.dot_general(hot, rows, TN, preferred_element_type=F32).astype(BF16)
@@ -1354,7 +1360,7 @@
         pltpu.VMEM((2, *part_b), BF16),
         pltpu.VMEM(part_b[2:], BF16),
         pltpu.VMEM(part_b[2:], BF16),
-        DMA((7,)),
+        DMA((9,)),
     ]
     scratch += [DMA((1,))] * 2
     scratch += [DMA((n,))] * 8

time: 70.8 us -> 70.8 us (level)
  no operation moved by 1% of the time
where the time goes in v5:
time: 70.8 us; the launch traced here: 70.6 us
  Pallas kernels  69.3 us (98%)
  between operations  1.29 us (2%)
    pallas_call x1, Pallas kernels, fused(): pl.pallas_call(functools.partial(fused_kernel, n), out_shape=(row, row, j...  67.3 us
    pallas_call x1, Pallas kernels, finish(): pl.pallas_call(finish_kernel, out_shape=(jax.ShapeDtypeStruct((1, *emb.sh...  1.97 us

profile of v5, /device:TPU:0, one launch (start us, length us, event | category | flops | bytes accessed | tf_op | source)
XLA Modules:
  0.0 70.6 jit_solution(14296389939032053363)
XLA Ops:
  1.3 67.3 %shard_map.103 = (bf16[256,768]{1,0:T(8,128)(2,1)S(1)}, bf16[256,768]{1,0:T(8,128)(2,1)S(1)}, bf16[2,2,4,128,384]{4,3,2,1,0:T(8,128)(2,1)S(1)}) custom-call(bf16[512,2048]{1,0:T(8,128)(2,1)} %feats_hbm.1, s32[1,512]{1,0:T(1,128)} %pos_hbm.1, s32[1,128]{1,0:T(1,128)S(1)} %broadcast_in_dim.9.slide_count, bf16[2048,384]{1,0:T(8,128)(2,1)} %wproj_hbm.1, ...), custom_call_target="tpu_custom_call" | custom-call | flops 5000000000 | bytes 10000000 | tf_op jit(solution)/shard_map/pallas_call | solution.py:1382
  68.6 2.0 %shard_map.104 = (bf16[1,256,768]{2,1,0:T(8,128)(2,1)}, bf16[1,256,768]{2,1,0:T(8,128)(2,1)}, f32[2048,384]{1,0:T(8,128)}) custom-call(bf16[256,768]{1,0:T(8,128)(2,1)S(1)} %get-tuple-element.6.emb, bf16[256,768]{1,0:T(8,128)(2,1)S(1)} %get-tuple-element.7.branch, bf16[2048,384]{1,0:T(8,128)(2,1)S(1)} %bitcast.3), custom_call_target="tpu_custom_call" | custom-call | bytes 6000000 | tf_op jit(solution)/shard_map/pallas_call | solution.py:1302
  (1 shorter events, 0.0 us)
